TPU v7x, 32 devices: a whole 2x2x4 slice. The times are simulated.
32 devices in a mesh: section: 4 (over y, core), blk: 2 (over x), head: 4 (over z).
Axes of the slice: x: 2, y: 2, z: 4, core: 2. Of those that a mesh axis runs over, the one named last changes fastest.
Arguments:
- queries: bfloat16 [4, 512, 2048], P('section', ('blk', 'head')), may hold values from -24 to 24
- keys_values: bfloat16 [4, 512, 1024], P('section', ('blk', 'head')), may hold values from -8 to 8
- segment_ids: int32 [4, 512], P('section', ('blk', 'head')), may hold values from 0 to 3, never falling along the last dimension, each value on 1 to 384 neighbouring positions
Outputs:
- attended: bfloat16 [4, 512, 2048], P('section', ('blk', 'head'))
All inputs are finite; a program needn't handle non-finite values.
Results may differ from a plain program's by a relative error of at most 0.004.
Values may be sent and summed in bfloat16 or wider, within the bound.
A program may use at most 64 MiB of HBM per device.

v0:
```python
import math

import jax
import jax.numpy as jnp
from jax import lax
from jax.sharding import PartitionSpec as P

HEAD_SIZE = 128


NEG_FILL = -1e30
ROW_GROUPS = 4


def from_behind(block, axis, distance):
    devices = range(lax.axis_size(axis))
    route = [((i - distance) % len(devices), i) for i in devices]
    return lax.ppermute(block, axis, route)


def update_group(
    carried, query_group, place_group, label_group, key_rows, value_rows, key_places, key_labels
):
    accumulated, running_top, running_total = carried
    scores = jnp.einsum("rkgd,skd->kgrs", query_group, key_rows, preferred_element_type=jnp.float32)
    scores = scores / math.sqrt(query_group.shape[-1])
    allowed = (key_places[None, :] <= place_group[:, None]) & (
        key_labels[None, :] == label_group[:, None]
    )
    scores = jnp.where(allowed, scores, NEG_FILL)
    new_top = jnp.maximum(running_top, jnp.max(scores, axis=-1))
    weights = jnp.where(allowed, jnp.exp(scores - new_top[..., None]), 0.0)
    factor = jnp.exp(running_top - new_top)
    running_total = running_total * factor + jnp.sum(weights, axis=-1)
    accumulated = accumulated * factor[..., None] + jnp.einsum(
        "kgrs,skd->kgrd",
        weights.astype(jnp.bfloat16),
        value_rows,
        preferred_element_type=jnp.float32,
    )
    return (accumulated, new_top, running_total)


def keep_group(
    carried, query_group, place_group, label_group, key_rows, value_rows, key_places, key_labels
):
    return carried


def attend_rows(query_rows, query_places, query_labels, grouped_key_heads, gather_keys):
    rows = query_rows.shape[0]
    query_heads = query_rows.shape[1] // HEAD_SIZE
    grouped = query_heads // grouped_key_heads
    group_rows = rows // ROW_GROUPS
    shaped = query_rows.reshape(ROW_GROUPS, group_rows, grouped_key_heads, grouped, HEAD_SIZE)
    places = query_places.reshape(ROW_GROUPS, group_rows)
    labels = query_labels.reshape(ROW_GROUPS, group_rows)
    initial = tuple(
        (
            (
                jnp.zeros((grouped_key_heads, grouped, group_rows, HEAD_SIZE), jnp.float32),
                jnp.full((grouped_key_heads, grouped, group_rows), NEG_FILL, jnp.float32),
                jnp.zeros((grouped_key_heads, grouped, group_rows), jnp.float32),
            )
            for which in range(ROW_GROUPS)
        )
    )

    def fold_keys(carried, piece, start):
        pair_piece, label_piece = piece
        token_length = pair_piece.shape[1]
        results = carried
        for offset in range(0, token_length, 512):
            width = min(512, token_length - offset)
            block = pair_piece[0, offset : offset + width].reshape(
                width, grouped_key_heads, 2, HEAD_SIZE
            )
            block_labels = label_piece[0, offset : offset + width]
            key_start = start + offset
            key_places = key_start + jnp.arange(width, dtype=jnp.int32)
            key_rows = block[:, :, 0, :]
            value_rows = block[:, :, 1, :]
            updated = []
            for which in range(ROW_GROUPS):
                needed = jnp.logical_and(
                    key_start <= jnp.max(places[which]), block_labels[-1] >= jnp.min(labels[which])
                )
                updated.append(
                    lax.cond(
                        needed,
                        update_group,
                        keep_group,
                        results[which],
                        shaped[which],
                        places[which],
                        labels[which],
                        key_rows,
                        value_rows,
                        key_places,
                        block_labels,
                    )
                )
            results = tuple(updated)
        return results

    final = gather_keys(fold_keys, initial)
    pieces = []
    for which in range(ROW_GROUPS):
        accumulated, running_top, running_total = final[which]
        normed = accumulated / running_total[..., None]
        pieces.append(normed.transpose(2, 0, 1, 3).reshape(group_rows, query_heads * HEAD_SIZE))
    return jnp.concatenate(pieces, axis=0).astype(jnp.bfloat16)


def per_device(queries, keys_values, segment_ids):
    head_count = lax.axis_size("head")
    labels = segment_ids.astype(jnp.bfloat16)
    queries, keys_values, labels = from_behind((queries, keys_values, labels), "section", 1)
    label_columns = jnp.broadcast_to(labels[:, :, None], labels.shape + (head_count,))
    local_queries, local_pairs, label_columns = (
        lax.all_to_all(queries, "head", split_axis=2, concat_axis=1, tiled=True),
        lax.all_to_all(keys_values, "head", split_axis=2, concat_axis=1, tiled=True),
        lax.all_to_all(label_columns, "head", split_axis=2, concat_axis=1, tiled=True),
    )
    rows = local_queries.shape[1]
    key_labels = label_columns[:, :, 0]
    block_index = lax.axis_index("blk")
    grouped_key_heads = local_pairs.shape[2] // (2 * HEAD_SIZE)
    query_places = block_index * rows + jnp.arange(rows, dtype=jnp.int32)
    query_rows = local_queries[0]
    query_labels = key_labels[0]

    def gather_blocks(fold_keys, initial):
        return fold_keys(
            initial,
            (
                lax.all_gather(local_pairs, "blk", axis=1, tiled=True),
                lax.all_gather(key_labels, "blk", axis=1, tiled=True),
            ),
            jnp.int32(0),
        )

    result = attend_rows(query_rows, query_places, query_labels, grouped_key_heads, gather_blocks)[
        None
    ]
    return lax.all_to_all(result, "head", split_axis=1, concat_axis=2, tiled=True)


def solution(mesh):
    return jax.shard_map(
        per_device,
        mesh=mesh,
        in_specs=(
            P("section", ("blk", "head"), None),
            P("section", ("blk", "head"), None),
            P("section", ("blk", "head")),
        ),
        out_specs=P("section", ("blk", "head"), None),
        check_vma=False,
    )
```

profile of v0, /device:TPU:0, one launch (start us, length us, event | category | flops | bytes accessed | tf_op | source)
XLA Modules:
  0.0 82.7 jit_solution(10671842217919871959)
XLA Ops:
  0.0 0.5 collective-permute-start.1
  0.5 0.7 convert_element_type.35
  1.1 2.6 %collective-permute-start = (bf16[1,64]{1,0:T(2,128)(2,1)S(1)}, bf16[1,64]{1,0:T(2,128)(2,1)S(1)}, u32[]{:S(2)}, u32[]{:S(2)}) collective-permute-start(bf16[1,64]{1,0:T(2,128)(2,1)S(1)} %convert_element_type.35), channel_id=1, source_target_pairs={{24,0},{0,8},{8,16},{16,24},{25,1},{1,9},{9,17},{17,25},{26,2},{2,... | collective-permute-start | bytes 392 | tf_op jit(solution)/shard_map/ppermute | solution.py:18
  3.7 0.0 collective-permute-start.2
  3.7 1.6 %collective-permute-done = bf16[1,64]{1,0:T(2,128)(2,1)S(1)} collective-permute-done((bf16[1,64]{1,0:T(2,128)(2,1)S(1)}, bf16[1,64]{1,0:T(2,128)(2,1)S(1)}, u32[]{:S(2)}, u32[]{:S(2)}) %collective-permute-start) | collective-permute-done | bytes 160 | tf_op jit(solution)/shard_map/ppermute | solution.py:18
  5.3 0.6 broadcast_in_dim.68
  5.9 5.7 %all-to-all-start = ((bf16[1,64,4]{1,0,2:T(2,128)(2,1)}), bf16[1,64,4]{1,0,2:T(2,128)(2,1)S(1)}, u32[]{:S(2)}, u32[]{:S(2)}) async-start(bf16[1,64,4]{1,0,2:T(2,128)(2,1)} %broadcast_in_dim.68), calls=%async_computation | async-start | bytes 4096 | tf_op jit(solution)/shard_map/all_to_all | solution.py:123
  11.6 0.4 copy.92
  12.0 0.5 broadcast.345
  12.5 2.2 %reduce.20 = bf16[1024,64]{1,0:T(8,128)(2,1)S(1)} reduce(bf16[1024,1,64]{2,1,0:T(2,128)(2,1)S(1)} %bitcast.177, bf16[]{:T(256)} %broadcast.345), dimensions={1}, to_apply=%bitcast.153.reduce_sub_computation | reduce | bytes 262146
  14.7 0.9 %reshape.440 = bf16[4,2,8192]{2,1,0:T(2,128)(2,1)} reshape(bf16[1024,64]{1,0:T(8,128)(2,1)S(1)} %reduce.20) | data formatting | bytes 262144
  15.6 1.5 %all-to-all-done = bf16[1,64,4]{1,0,2:T(2,128)(2,1)S(1)} async-done(((bf16[1,64,4]{1,0,2:T(2,128)(2,1)}), bf16[1,64,4]{1,0,2:T(2,128)(2,1)S(1)}, u32[]{:S(2)}, u32[]{:S(2)}) %all-to-all-start) | async-done | bytes 544 | tf_op jit(solution)/shard_map/all_to_all | solution.py:123
  17.0 3.6 %all-to-all-start.1 = ((bf16[4,2,8192]{2,1,0:T(2,128)(2,1)}), bf16[4,2,8192]{2,1,0:T(2,128)(2,1)S(1)}, u32[]{:S(2)}, u32[]{:S(2)}) async-start(bf16[4,2,8192]{2,1,0:T(2,128)(2,1)} %reshape.440), calls=%async_computation.1 | async-start | bytes 262144 | tf_op jit(solution)/shard_map/all_to_all | solution.py:122
  20.6 0.8 slice_reduce_fusion.7
  24.0 0.7 copy.96
  24.8 11.5 %reduce.21 = bf16[2048,64]{1,0:T(8,128)(2,1)S(1)} reduce(bf16[2048,1,64]{2,1,0:T(2,128)(2,1)S(1)} %bitcast.175, bf16[]{:T(256)} %broadcast.345), dimensions={1}, to_apply=%bitcast.155.reduce_sub_computation | reduce | bytes 524290
  36.2 1.1 %reshape.442 = bf16[4,2,16384]{2,1,0:T(2,128)(2,1)} reshape(bf16[2048,64]{1,0:T(8,128)(2,1)S(1)} %reduce.21) | data formatting | bytes 524288
  37.3 5.1 %all-to-all-start.2 = ((bf16[4,2,16384]{2,1,0:T(2,128)(2,1)}), bf16[4,2,16384]{2,1,0:T(2,128)(2,1)S(1)}, u32[]{:S(2)}, u32[]{:S(2)}) async-start(bf16[4,2,16384]{2,1,0:T(2,128)(2,1)} %reshape.442), calls=%async_computation.2 | async-start | bytes 524288 | tf_op jit(solution)/shard_map/all_to_all | solution.py:121
  42.4 0.7 slice_reduce_fusion.6
  43.1 0.1 squeeze.12
  43.2 4.2 %all_gather.6 = bf16[1,512]{1,0:T(2,128)(2,1)S(1)} all-gather(bf16[1,256]{1,0:T(2,128)(2,1)S(1)} %squeeze.12), channel_id=1, replica_groups=mesh['section'=4,'blk'=2,'head'=4] {'blk'}, dimensions={1}, use_global_device_ids=true | all-gather | bytes 1536 | tf_op jit(solution)/shard_map/all_gather | solution.py:138
  47.4 0.7 slice.88
  53.3 0.3 reshape.441
  53.6 0.3 copy.93
  54.0 0.1 all_to_all.52
  54.1 5.6 %all_gather.7 = bf16[1,512,256]{2,1,0:T(8,128)(2,1)S(1)} all-gather(bf16[1,256,256]{2,1,0:T(8,128)(2,1)S(1)} %bitcast.182), channel_id=1, replica_groups=mesh['section'=4,'blk'=2,'head'=4] {'blk'}, dimensions={1}, use_global_device_ids=true | all-gather | bytes 393216 | tf_op jit(solution)/shard_map/all_gather | solution.py:137
  59.7 0.1 copy.95
  59.9 0.6 reshape.443
  60.6 0.6 copy.97
  61.2 0.2 all_to_all.56
  61.4 1.1 %conditional.4 = (f32[1,4,64,128]{3,2,1,0:T(8,128)S(1)}, f32[1,4,64]{2,1,0:T(4,128)S(1)}) conditional(s32[]{:T(128)} %convert_element_type.36, () %tuple.37, (s32[512]{0:T(512)S(1)}, s32[64]{0:T(128)S(1)}, bf16[1,512]{1,0:T(2,128)(2,1)S(1)}, bf16[1,1,64,1]{2,1,3,0:T(2,128)(2,1)S(1)}, bf16[512,1,128]{0,2,1:T(8,128)(2,1)S(1)}, ...), branch_computations={%region_2.0_spmd, %region_3.6_spmd} | conditional | flops 68485888 | bytes 2965906 | solution.py:89
  61.4 0.1 compare_and_fusion
  61.6 0.3 fusion.60
  61.9 0.2 fusion.3
  62.2 0.3 fusion.2
  62.5 0.1 fusion.56
  62.6 0.1 copy.102
  62.7 1.1 %conditional.5 = (f32[1,4,64,128]{3,2,1,0:T(8,128)S(1)}, f32[1,4,64]{2,1,0:T(4,128)S(1)}) conditional(s32[]{:T(128)} %convert_element_type.37, () %tuple.39, (s32[512]{0:T(512)S(1)}, s32[64]{0:T(128)S(1)}, bf16[1,512]{1,0:T(2,128)(2,1)S(1)}, bf16[1,1,64,1]{2,1,3,0:T(2,128)(2,1)S(1)}, bf16[512,1,128]{0,2,1:T(8,128)(2,1)S(1)}, ...), branch_computations={%region_8.9_spmd, %region_9.12_spmd} | conditional | flops 68485888 | bytes 2965906 | solution.py:89
  62.7 0.1 compare_and_fusion.1
  62.9 0.3 fusion.61
  63.2 0.2 fusion.17
  63.5 0.3 fusion.16
  63.8 0.1 fusion.57
  63.9 0.1 copy.107
  64.0 1.3 %conditional.6 = (f32[1,4,64,128]{3,2,1,0:T(8,128)S(1)}, f32[1,4,64]{2,1,0:T(4,128)S(1)}) conditional(s32[]{:T(128)} %convert_element_type.38, () %tuple.41, (s32[512]{0:T(512)S(1)}, s32[64]{0:T(128)S(1)}, bf16[1,512]{1,0:T(2,128)(2,1)S(1)}, bf16[1,1,64,1]{2,1,3,0:T(2,128)(2,1)S(1)}, bf16[512,1,128]{0,2,1:T(8,128)(2,1)S(1)}, ...), branch_computations={%region_14.15_spmd, %region_15.18_spmd} | conditional | flops 68485888 | bytes 2965906 | solution.py:89
  64.2 0.1 compare_and_fusion.2
  64.4 0.3 fusion.62
  64.7 0.2 fusion.31
  65.0 0.3 fusion.30
  65.3 0.1 fusion.58
  65.4 0.1 copy.112
  65.5 1.1 %conditional.7 = (f32[1,4,64,128]{3,2,1,0:T(8,128)S(1)}, f32[1,4,64]{2,1,0:T(4,128)S(1)}) conditional(s32[]{:T(128)} %convert_element_type.39, () %tuple.43, (s32[512]{0:T(512)S(1)}, s32[64]{0:T(128)S(1)}, bf16[1,512]{1,0:T(2,128)(2,1)S(1)}, bf16[1,1,64,1]{2,1,3,0:T(2,128)(2,1)S(1)}, bf16[512,1,128]{0,2,1:T(8,128)(2,1)S(1)}, ...), branch_computations={%region_20.21_spmd, %region_21.24_spmd} | conditional | flops 68485888 | bytes 2965906 | solution.py:89
  65.6 0.1 compare_and_fusion.3
  65.8 0.3 fusion.63
  66.1 0.2 fusion.45
  66.3 0.3 fusion.44
  66.6 0.1 fusion.59
  66.7 0.1 copy.117
  66.9 0.4 copy.142
  67.3 2.1 %reduce.22 = bf16[256,512]{1,0:T(8,128)(2,1)S(1)} reduce(bf16[256,1,512]{2,1,0:T(2,128)(2,1)S(1)} %bitcast.179, bf16[]{:T(256)} %broadcast.345), dimensions={1}, to_apply=%bitcast.169.reduce_sub_computation | reduce | bytes 524290
  69.4 0.2 reshape.444
  69.6 12.0 %all_to_all.66 = bf16[4,2,16384]{2,1,0:T(2,128)(2,1)S(1)} all-to-all(bf16[4,2,16384]{2,1,0:T(2,128)(2,1)S(1)} %reshape.444), channel_id=1, replica_groups=mesh['section'=4,'blk'=2,'head'=4] {'head'}, dimensions={0} | all-to-all | bytes 524288 | tf_op jit(solution)/shard_map/all_to_all | solution.py:146
  81.6 0.3 reshape.445
  81.9 0.7 copy.122
  (42 shorter events, 0.7 us)
Async XLA Ops:
  0.0 11.6 %collective-permute-start.1 = (bf16[1,64,1024]{2,1,0:T(8,128)(2,1)}, bf16[1,64,1024]{2,1,0:T(8,128)(2,1)S(1)}, u32[]{:S(2)}, u32[]{:S(2)}) collective-permute-start(bf16[1,64,1024]{2,1,0:T(8,128)(2,1)} %param.12), channel_id=1, source_target_pairs={{24,0},{0,8},{8,16},{16,24},{25,1},{1,9},{9,17},{17,25},{26,2},{2,... | collective-permute-start | bytes 393224 | tf_op jit(solution)/shard_map/ppermute | solution.py:18
  1.1 4.2 %collective-permute-start = (bf16[1,64]{1,0:T(2,128)(2,1)S(1)}, bf16[1,64]{1,0:T(2,128)(2,1)S(1)}, u32[]{:S(2)}, u32[]{:S(2)}) collective-permute-start(bf16[1,64]{1,0:T(2,128)(2,1)S(1)} %convert_element_type.35), channel_id=1, source_target_pairs={{24,0},{0,8},{8,16},{16,24},{25,1},{1,9},{9,17},{17,25},{26,2},{2,... | collective-permute-start | bytes 392 | tf_op jit(solution)/shard_map/ppermute | solution.py:18
  3.7 20.3 %collective-permute-start.2 = (bf16[1,64,2048]{2,1,0:T(8,128)(2,1)}, bf16[1,64,2048]{2,1,0:T(8,128)(2,1)S(1)}, u32[]{:S(2)}, u32[]{:S(2)}) collective-permute-start(bf16[1,64,2048]{2,1,0:T(8,128)(2,1)} %param.11), channel_id=1, source_target_pairs={{24,0},{0,8},{8,16},{16,24},{25,1},{1,9},{9,17},{17,25},{26,2},{2,... | collective-permute-start | bytes 786440 | tf_op jit(solution)/shard_map/ppermute | solution.py:18
  5.9 11.1 %all-to-all-start = ((bf16[1,64,4]{1,0,2:T(2,128)(2,1)}), bf16[1,64,4]{1,0,2:T(2,128)(2,1)S(1)}, u32[]{:S(2)}, u32[]{:S(2)}) async-start(bf16[1,64,4]{1,0,2:T(2,128)(2,1)} %broadcast_in_dim.68), calls=%async_computation | async-start | bytes 4096 | tf_op jit(solution)/shard_map/all_to_all | solution.py:123
  17.0 20.3 %all-to-all-start.1 = ((bf16[4,2,8192]{2,1,0:T(2,128)(2,1)}), bf16[4,2,8192]{2,1,0:T(2,128)(2,1)S(1)}, u32[]{:S(2)}, u32[]{:S(2)}) async-start(bf16[4,2,8192]{2,1,0:T(2,128)(2,1)} %reshape.440), calls=%async_computation.1 | async-start | bytes 262144 | tf_op jit(solution)/shard_map/all_to_all | solution.py:122
  37.3 22.6 %all-to-all-start.2 = ((bf16[4,2,16384]{2,1,0:T(2,128)(2,1)}), bf16[4,2,16384]{2,1,0:T(2,128)(2,1)S(1)}, u32[]{:S(2)}, u32[]{:S(2)}) async-start(bf16[4,2,16384]{2,1,0:T(2,128)(2,1)} %reshape.442), calls=%async_computation.2 | async-start | bytes 524288 | tf_op jit(solution)/shard_map/all_to_all | solution.py:121
where the time goes:
time: 83.2 us; the launch traced here: 82.7 us
  blocking collectives  21.9 us (26%)
  other arithmetic  19.8 us (24%)
  starting transfers between devices  17.4 us (21%)
  local copies, waits for them, and re-layouts  9.54 us (11%)
  between operations  8.12 us (10%)
  waiting for transfers between devices  3.07 us (4%)
  matrix products  2.32 us (3%)
    unnamed x3, other arithmetic  15.8 us
    all_to_all x1, blocking collectives, per_device(): lax.all_to_all(result, 'head', split_axis=1, concat_axis=2, tiled=True)  12 us
    all_to_all x1, starting transfers between devices, per_device(): lax.all_to_all(label_columns, 'head', split_axis=2, concat_axis=1, tiled=...  5.65 us
    all_gather x1, blocking collectives, gather_blocks(): lax.all_gather(local_pairs, 'blk', axis=1, tiled=True)  5.64 us
    all_to_all x1, starting transfers between devices, per_device(): lax.all_to_all(queries, 'head', split_axis=2, concat_axis=1, tiled=True)  5.09 us
    all_gather x1, blocking collectives, gather_blocks(): lax.all_gather(key_labels, 'blk', axis=1, tiled=True)  4.23 us
    unnamed x9, local copies, waits for them, and re-layouts  3.94 us
    all_to_all x1, starting transfers between devices, per_device(): lax.all_to_all(keys_values, 'head', split_axis=2, concat_axis=1, tiled=True)  3.6 us
  transfers between devices with their start and end apart: 6, of which 2 were waited for; matrix products, arithmetic and copies ran while one was open for 26% of the time, Pallas kernels for 0%

commit v1 on v0

v1 whole, which is shorter than its diff:
```python
import functools
import math

import jax
import jax.numpy as jnp
from jax import lax
from jax.experimental import pallas as pl
from jax.experimental.pallas import tpu as pltpu
from jax.sharding import PartitionSpec as P

HEAD_SIZE = 128
MASKED = -1e30
MESH = pl.DeviceIdType.MESH
RIGHT, DOWN, LEFT, OWN = range(4)


def kernel(
    sections, blocks, columns, q_in, kv_in, seg_in, out_ref,
    q, kv, seg, q_send, q_recv, kv_send, kv_recv, seg_send, seg_recv,
):
    s, x, z = lax.axis_index("section"), lax.axis_index("blk"), lax.axis_index("head")
    after, before = lax.rem(s + 1, sections), lax.rem(s + sections - 1, sections)
    rows = q.shape[0]
    me = x * columns + z
    count = blocks * columns
    has_right, has_left = z < columns - 1, z > 0
    has_down, has_up = x < blocks - 1, x > 0
    below = x > 0

    barrier = pltpu.get_barrier_semaphore()

    def greet(section, blk, head):
        pl.semaphore_signal(barrier, inc=1, device_id=(section, blk, head), device_id_type=MESH)

    greet(before, x, z)

    @pl.when(has_left)
    def _():
        greet(before, x, z - 1)
        greet(s, x, z - 1)

    @pl.when(has_up)
    def _():
        greet(before, x - 1, z)
        greet(s, x - 1, z)

    @pl.when(jnp.logical_and(below, has_right))
    def _():
        greet(s, x, z + 1)

    one = lambda c: jnp.where(c, 1, 0)
    pl.semaphore_wait(
        barrier,
        1 + 2 * one(has_right) + 2 * one(has_down) + one(jnp.logical_and(below, has_left)),
    )

    def copies(way, slot, device, first):
        src_kv, src_seg = (kv_in.at[0], seg_in) if first else (kv.at[slot], seg.at[slot])
        return (
            pltpu.make_async_remote_copy(
                src_ref=src_kv, dst_ref=kv.at[slot], send_sem=kv_send.at[way, slot],
                recv_sem=kv_recv.at[slot], device_id=device, device_id_type=MESH,
            ),
            pltpu.make_async_remote_copy(
                src_ref=src_seg, dst_ref=seg.at[slot], send_sem=seg_send.at[way, slot],
                recv_sem=seg_recv.at[slot], device_id=device, device_id_type=MESH,
            ),
        )

    def walk(act, wait):
        def passing(condition, way, slot, device, first=False):
            @pl.when(condition)
            def _():
                for copy in copies(way, slot, device, first):
                    act(copy)

        passing(has_right, RIGHT, me, (after, x, z + 1), True)
        passing(has_down, DOWN, me, (after, x + 1, z), True)
        for copy in copies(OWN, me, (after, x, z), True):
            act(copy)
        act(
            pltpu.make_async_remote_copy(
                src_ref=q_in.at[0], dst_ref=q, send_sem=q_send, recv_sem=q_recv,
                device_id=(after, x, z), device_id_type=MESH,
            )
        )
        for d in range(columns):
            if d > 0:
                @pl.when(z >= d)
                def _():
                    slot = me - d
                    wait(slot)
                    passing(has_right, RIGHT, slot, (s, x, z + 1))
                    passing(has_down, DOWN, slot, (s, x + 1, z))
            for e in range(1, blocks):
                @pl.when(jnp.logical_and(x >= e, z >= d))
                def _():
                    slot = me - e * columns - d
                    wait(slot)
                    passing(has_down, DOWN, slot, (s, x + 1, z))
                    if d == 0:
                        passing(has_left, LEFT, slot, (s, x, z - 1))
                if d > 0:
                    @pl.when(jnp.logical_and(x >= e, z + d < columns))
                    def _():
                        slot = me - e * columns + d
                        wait(slot)
                        passing(has_left, LEFT, slot, (s, x, z - 1))

    def wait_slot(slot):
        for copy in copies(OWN, slot, (after, x, z), False):
            copy.wait_recv()

    for slot in range(1, count):
        @pl.when(slot > me)
        def _():
            kv[slot] = jnp.zeros(kv.shape[1:], kv.dtype)
            seg[slot] = jnp.zeros(seg.shape[1:], seg.dtype)

    walk(lambda copy: copy.start(), wait_slot)
    wait_slot(me)
    pltpu.make_async_remote_copy(
        src_ref=q, dst_ref=q, send_sem=q_send, recv_sem=q_recv,
        device_id=(after, x, z), device_id_type=MESH,
    ).wait_recv()

    span = count * rows
    key_labels = jnp.concatenate([seg[slot] for slot in range(count)], axis=1)
    own = jnp.broadcast_to(seg[me], (rows, rows))
    diagonal = lax.broadcasted_iota(jnp.int32, (rows, rows), 0) == lax.broadcasted_iota(
        jnp.int32, (rows, rows), 1
    )
    query_labels = jnp.sum(jnp.where(diagonal, own, 0), axis=1, keepdims=True)
    places = lax.broadcasted_iota(jnp.int32, (rows, span), 0) + me * rows
    allowed = jnp.logical_and(
        lax.broadcasted_iota(jnp.int32, (rows, span), 1) <= places, key_labels == query_labels
    )
    query_heads = q.shape[1] // HEAD_SIZE
    key_heads = kv.shape[2] // (2 * HEAD_SIZE)
    group = query_heads // key_heads
    factor = math.log2(math.e) / math.sqrt(HEAD_SIZE)
    bias = jnp.where(allowed, 0.0, MASKED)
    bias = jnp.concatenate([bias] * group, axis=0)
    for k in range(key_heads):
        at = 2 * k * HEAD_SIZE
        keys = kv[:, :, at : at + HEAD_SIZE].reshape(span, HEAD_SIZE)
        values = kv[:, :, at + HEAD_SIZE : at + 2 * HEAD_SIZE].reshape(span, HEAD_SIZE)
        queries = jnp.concatenate(
            [q[:, h * HEAD_SIZE : (h + 1) * HEAD_SIZE] for h in range(group * k, group * (k + 1))], axis=0
        )
        scores = lax.dot_general(
            queries, keys, (((1,), (1,)), ((), ())), preferred_element_type=jnp.float32
        ) + bias
        top = jnp.max(scores, axis=1, keepdims=True)
        weights = jnp.exp2((scores - top) * factor)
        total = jnp.sum(weights, axis=1, keepdims=True)
        mixed = jnp.dot(weights.astype(jnp.bfloat16), values, preferred_element_type=jnp.float32) / total
        mixed = mixed.astype(jnp.bfloat16)
        for g in range(group):
            h = group * k + g
            out_ref[0, :, h * HEAD_SIZE : (h + 1) * HEAD_SIZE] = mixed[g * rows : (g + 1) * rows]

    walk(lambda copy: copy.wait_send(), lambda slot: None)


def per_device(queries, keys_values, segment_ids):
    sections, blocks, columns = (lax.axis_size(a) for a in ("section", "blk", "head"))
    rows = queries.shape[1]
    count = blocks * columns
    return pl.pallas_call(
        functools.partial(kernel, sections, blocks, columns),
        out_shape=jax.ShapeDtypeStruct(queries.shape, jnp.bfloat16),
        in_specs=[pl.BlockSpec(memory_space=pl.ANY)] * 3,
        out_specs=pl.BlockSpec(memory_space=pltpu.VMEM),
        scratch_shapes=[
            pltpu.VMEM(queries.shape[1:], jnp.bfloat16),
            pltpu.VMEM((count,) + keys_values.shape[1:], jnp.bfloat16),
            pltpu.VMEM((count, 1, rows), jnp.int32),
            pltpu.SemaphoreType.DMA,
            pltpu.SemaphoreType.DMA,
            pltpu.SemaphoreType.DMA((4, count)),
            pltpu.SemaphoreType.DMA((count,)),
            pltpu.SemaphoreType.DMA((4, count)),
            pltpu.SemaphoreType.DMA((count,)),
        ],
        compiler_params=pltpu.CompilerParams(
            collective_id=0, has_side_effects=True, vmem_limit_bytes=48 * 1024 * 1024
        ),
    )(queries, keys_values, segment_ids)


def solution(mesh):
    return jax.shard_map(
        per_device,
        mesh=mesh,
        in_specs=(
            P("section", ("blk", "head"), None),
            P("section", ("blk", "head"), None),
            P("section", ("blk", "head")),
        ),
        out_specs=P("section", ("blk", "head"), None),
        check_vma=False,
    )
```

time: 83.2 us -> 26.3 us (0.32)
  the two profiles are of different devices: /device:TPU:0 before, /device:TPU:2 now
where the time goes in v1:
time: 26.3 us; the launch traced here: 26.1 us
  Pallas kernels  22.9 us (87%)
  local copies, waits for them, and re-layouts  3.21 us (12%)
    pallas_call x1, Pallas kernels, per_device(): pl.pallas_call(functools.partial(kernel, sections, blocks, columns), out_...  22.9 us
    unnamed x7, local copies, waits for them, and re-layouts  3.21 us

profile of v1, /device:TPU:2, one launch (start us, length us, event | category | flops | bytes accessed | tf_op | source)
XLA Modules:
  0.0 26.1 jit_solution(11232538410668968749)
XLA Ops:
  0.0 0.0 copy-start
  0.0 0.9 %copy-done = bf16[1,64,2048]{2,1,0:T(8,128)(2,1)S(1)} copy-done((bf16[1,64,2048]{2,1,0:T(8,128)(2,1)S(1)}, bf16[1,64,2048]{2,1,0:T(8,128)(2,1)}, u32[]{:S(2)}) %copy-start) | copy-done | bytes 262168
  1.0 0.0 copy-start.1
  1.0 0.9 %copy-done.1 = bf16[1,64,1024]{2,1,0:T(8,128)(2,1)S(1)} copy-done((bf16[1,64,1024]{2,1,0:T(8,128)(2,1)S(1)}, bf16[1,64,1024]{2,1,0:T(8,128)(2,1)}, u32[]{:S(2)}) %copy-start.1) | copy-done | bytes 131096
  1.9 0.0 copy-start.2
  1.9 0.7 %copy-done.2 = s32[1,64]{1,0:T(1,128)S(1)} copy-done((s32[1,64]{1,0:T(1,128)S(1)}, s32[1,64]{1,0:T(1,128)}, u32[]{:S(2)}) %copy-start.2) | copy-done | bytes 280
  2.5 22.9 %shard_map.37 = bf16[1,64,2048]{2,1,0:T(8,128)(2,1)S(1)} custom-call(bf16[1,64,2048]{2,1,0:T(8,128)(2,1)S(1)} %copy-done, bf16[1,64,1024]{2,1,0:T(8,128)(2,1)S(1)} %copy-done.1, s32[1,64]{1,0:T(1,128)S(1)} %copy-done.2), custom_call_target="tpu_custom_call" | custom-call | tf_op jit(solution)/shard_map/pallas_call | solution.py:170
  25.4 0.7 %copy.5 = bf16[1,64,2048]{2,1,0:T(8,128)(2,1)} copy(bf16[1,64,2048]{2,1,0:T(8,128)(2,1)S(1)} %shard_map.37) | data formatting | bytes 524288
Async XLA Ops:
  0.0 0.9 %copy-start = (bf16[1,64,2048]{2,1,0:T(8,128)(2,1)S(1)}, bf16[1,64,2048]{2,1,0:T(8,128)(2,1)}, u32[]{:S(2)}) copy-start(bf16[1,64,2048]{2,1,0:T(8,128)(2,1)} %q_in.1) | copy-start | bytes 786436
  1.0 0.9 %copy-start.1 = (bf16[1,64,1024]{2,1,0:T(8,128)(2,1)S(1)}, bf16[1,64,1024]{2,1,0:T(8,128)(2,1)}, u32[]{:S(2)}) copy-start(bf16[1,64,1024]{2,1,0:T(8,128)(2,1)} %kv_in.1) | copy-start | bytes 393220
  1.9 0.7 %copy-start.2 = (s32[1,64]{1,0:T(1,128)S(1)}, s32[1,64]{1,0:T(1,128)}, u32[]{:S(2)}) copy-start(s32[1,64]{1,0:T(1,128)} %seg_in.1) | copy-start | bytes 772

commit v2 on v1

--- a/solution.py
+++ b/solution.py
@@ -12,6 +12,7 @@
 MASKED = -1e30
 MESH = pl.DeviceIdType.MESH
 RIGHT, DOWN, LEFT, OWN = range(4)
+PIECES = 2
 
 
 def kernel(
@@ -54,62 +55,84 @@
         1 + 2 * one(has_right) + 2 * one(has_down) + one(jnp.logical_and(below, has_left)),
     )
 
-    def copies(way, slot, device, first):
-        src_kv, src_seg = (kv_in.at[0], seg_in) if first else (kv.at[slot], seg.at[slot])
-        return (
-            pltpu.make_async_remote_copy(
-                src_ref=src_kv, dst_ref=kv.at[slot], send_sem=kv_send.at[way, slot],
-                recv_sem=kv_recv.at[slot], device_id=device, device_id_type=MESH,
-            ),
-            pltpu.make_async_remote_copy(
-                src_ref=src_seg, dst_ref=seg.at[slot], send_sem=seg_send.at[way, slot],
+    width = kv.shape[2] // PIECES
+
+    def copies(way, slot, piece, device, first=False):
+        part = pl.ds(piece * width, width)
+        src = kv_in.at[0, :, part] if first else kv.at[slot, :, part]
+        yield pltpu.make_async_remote_copy(
+            src_ref=src, dst_ref=kv.at[slot, :, part], send_sem=kv_send.at[way, slot, piece],
+            recv_sem=kv_recv.at[slot, piece], device_id=device, device_id_type=MESH,
+        )
+        if piece == 0:
+            yield pltpu.make_async_remote_copy(
+                src_ref=seg_in if first else seg.at[slot], dst_ref=seg.at[slot], send_sem=seg_send.at[way, slot],
                 recv_sem=seg_recv.at[slot], device_id=device, device_id_type=MESH,
-            ),
-        )
-
-    def walk(act, wait):
-        def passing(condition, way, slot, device, first=False):
-            @pl.when(condition)
-            def _():
-                for copy in copies(way, slot, device, first):
-                    act(copy)
-
-        passing(has_right, RIGHT, me, (after, x, z + 1), True)
-        passing(has_down, DOWN, me, (after, x + 1, z), True)
-        for copy in copies(OWN, me, (after, x, z), True):
-            act(copy)
-        act(
-            pltpu.make_async_remote_copy(
-                src_ref=q_in.at[0], dst_ref=q, send_sem=q_send, recv_sem=q_recv,
-                device_id=(after, x, z), device_id_type=MESH,
             )
-        )
+
+    def wait_piece(slot, piece):
+        for copy in copies(OWN, slot, piece, (after, x, z)):
+            copy.wait_recv()
+
+    def passing(condition, act, way, slot, piece, device, first=False):
+        @pl.when(condition)
+        def _():
+            for copy in copies(way, slot, piece, device, first):
+                act(copy)
+
+    def first_hops(act):
+        for piece in range(PIECES):
+            passing(has_right, act, RIGHT, me, piece, (after, x, z + 1), True)
+            passing(has_down, act, DOWN, me, piece, (after, x + 1, z), True)
+
+    query_copy = pltpu.make_async_remote_copy(
+        src_ref=q_in.at[0], dst_ref=q, send_sem=q_send, recv_sem=q_recv,
+        device_id=(after, x, z), device_id_type=MESH,
+    )
+
+    def own_hops(act):
+        for piece in range(PIECES):
+            for copy in copies(OWN, me, piece, (after, x, z), True):
+                act(copy)
+        act(query_copy)
+
+    def rounds(act, wait):
+        right, down, left = (s, x, z + 1), (s, x + 1, z), (s, x, z - 1)
         for d in range(columns):
-            if d > 0:
-                @pl.when(z >= d)
-                def _():
-                    slot = me - d
-                    wait(slot)
-                    passing(has_right, RIGHT, slot, (s, x, z + 1))
-                    passing(has_down, DOWN, slot, (s, x + 1, z))
-            for e in range(1, blocks):
-                @pl.when(jnp.logical_and(x >= e, z >= d))
-                def _():
-                    slot = me - e * columns - d
-                    wait(slot)
-                    passing(has_down, DOWN, slot, (s, x + 1, z))
-                    if d == 0:
-                        passing(has_left, LEFT, slot, (s, x, z - 1))
+            for piece in range(PIECES):
+                last = piece == PIECES - 1
                 if d > 0:
-                    @pl.when(jnp.logical_and(x >= e, z + d < columns))
+                    @pl.when(z >= d)
                     def _():
-                        slot = me - e * columns + d
-                        wait(slot)
-                        passing(has_left, LEFT, slot, (s, x, z - 1))
-
-    def wait_slot(slot):
-        for copy in copies(OWN, slot, (after, x, z), False):
-            copy.wait_recv()
+                        slot = me - d
+                        wait(slot, piece)
+                        passing(has_right, act, RIGHT, slot, piece, right)
+                        passing(jnp.logical_and(has_down, z > d) if last else has_down, act, DOWN, slot, piece, down)
+                for e in range(1, blocks):
+                    @pl.when(jnp.logical_and(x >= e, z >= d))
+                    def _():
+                        slot = me - e * columns - d
+                        wait(slot, piece)
+                        if d == 0:
+                            passing(has_left, act, LEFT, slot, piece, left)
+                            passing(has_down, act, DOWN, slot, piece, down)
+                        else:
+                            passing(
+                                jnp.logical_and(has_down, z > d) if last else has_down,
+                                act, DOWN, slot, piece, down,
+                            )
+                        if last:
+                            passing(jnp.logical_and(has_right, z == d), act, RIGHT, slot, piece, right)
+
+                    if d > 0:
+                        @pl.when(jnp.logical_and(x >= e, z + d < columns))
+                        def _():
+                            slot = me - e * columns + d
+                            wait(slot, piece)
+                            passing(has_left, act, LEFT, slot, piece, left)
+
+    start, sent = (lambda copy: copy.start()), (lambda copy: copy.wait_send())
+    first_hops(start)
 
     for slot in range(1, count):
         @pl.when(slot > me)
@@ -117,12 +140,12 @@
             kv[slot] = jnp.zeros(kv.shape[1:], kv.dtype)
             seg[slot] = jnp.zeros(seg.shape[1:], seg.dtype)
 
-    walk(lambda copy: copy.start(), wait_slot)
-    wait_slot(me)
-    pltpu.make_async_remote_copy(
-        src_ref=q, dst_ref=q, send_sem=q_send, recv_sem=q_recv,
-        device_id=(after, x, z), device_id_type=MESH,
-    ).wait_recv()
+    first_hops(sent)
+    own_hops(start)
+    rounds(start, wait_piece)
+    for piece in range(PIECES):
+        wait_piece(me, piece)
+    query_copy.wait_recv()
 
     span = count * rows
     key_labels = jnp.concatenate([seg[slot] for slot in range(count)], axis=1)
@@ -160,7 +183,8 @@
             h = group * k + g
             out_ref[0, :, h * HEAD_SIZE : (h + 1) * HEAD_SIZE] = mixed[g * rows : (g + 1) * rows]
 
-    walk(lambda copy: copy.wait_send(), lambda slot: None)
+    own_hops(sent)
+    rounds(sent, lambda slot, piece: None)
 
 
 def per_device(queries, keys_values, segment_ids):
@@ -170,7 +194,7 @@
     return pl.pallas_call(
         functools.partial(kernel, sections, blocks, columns),
         out_shape=jax.ShapeDtypeStruct(queries.shape, jnp.bfloat16),
-        in_specs=[pl.BlockSpec(memory_space=pl.ANY)] * 3,
+        in_specs=[pl.BlockSpec(memory_space=pltpu.HBM)] * 3,
         out_specs=pl.BlockSpec(memory_space=pltpu.VMEM),
         scratch_shapes=[
             pltpu.VMEM(queries.shape[1:], jnp.bfloat16),
@@ -178,8 +202,8 @@
             pltpu.VMEM((count, 1, rows), jnp.int32),
             pltpu.SemaphoreType.DMA,
             pltpu.SemaphoreType.DMA,
-            pltpu.SemaphoreType.DMA((4, count)),
-            pltpu.SemaphoreType.DMA((count,)),
+            pltpu.SemaphoreType.DMA((4, count, PIECES)),
+            pltpu.SemaphoreType.DMA((count, PIECES)),
             pltpu.SemaphoreType.DMA((4, count)),
             pltpu.SemaphoreType.DMA((count,)),
         ],

time: 26.3 us -> 24.5 us (0.932)
  Pallas kernels: 22.9 us -> 21.1 us
    pallas_call x1, Pallas kernels: 22.9 us -> 21.1 us  [per_device(): pl.pallas_call(functools.partial(kernel, sections, blocks, columns), out_...]
where the time goes in v2:
time: 24.5 us; the launch traced here: 24.3 us
  Pallas kernels  21.1 us (86%)
  local copies, waits for them, and re-layouts  3.21 us (13%)
    pallas_call x1, Pallas kernels, per_device(): pl.pallas_call(functools.partial(kernel, sections, blocks, columns), out_...  21.1 us
    unnamed x7, local copies, waits for them, and re-layouts  3.21 us

profile of v2, /device:TPU:2, one launch (start us, length us, event | category | flops | bytes accessed | tf_op | source)
XLA Modules:
  0.0 24.3 jit_solution(3320675926715364663)
XLA Ops:
  0.0 0.0 copy-start
  0.0 0.9 %copy-done = bf16[1,64,2048]{2,1,0:T(8,128)(2,1)S(1)} copy-done((bf16[1,64,2048]{2,1,0:T(8,128)(2,1)S(1)}, bf16[1,64,2048]{2,1,0:T(8,128)(2,1)}, u32[]{:S(2)}) %copy-start) | copy-done | bytes 262168
  1.0 0.0 copy-start.1
  1.0 0.9 %copy-done.1 = bf16[1,64,1024]{2,1,0:T(8,128)(2,1)S(1)} copy-done((bf16[1,64,1024]{2,1,0:T(8,128)(2,1)S(1)}, bf16[1,64,1024]{2,1,0:T(8,128)(2,1)}, u32[]{:S(2)}) %copy-start.1) | copy-done | bytes 131096
  1.9 0.0 copy-start.2
  1.9 0.7 %copy-done.2 = s32[1,64]{1,0:T(1,128)S(1)} copy-done((s32[1,64]{1,0:T(1,128)S(1)}, s32[1,64]{1,0:T(1,128)}, u32[]{:S(2)}) %copy-start.2) | copy-done | bytes 280
  2.5 21.1 %shard_map.37 = bf16[1,64,2048]{2,1,0:T(8,128)(2,1)S(1)} custom-call(bf16[1,64,2048]{2,1,0:T(8,128)(2,1)S(1)} %copy-done, bf16[1,64,1024]{2,1,0:T(8,128)(2,1)S(1)} %copy-done.1, s32[1,64]{1,0:T(1,128)S(1)} %copy-done.2), custom_call_target="tpu_custom_call" | custom-call | tf_op jit(solution)/shard_map/pallas_call | solution.py:194
  23.6 0.7 %copy.5 = bf16[1,64,2048]{2,1,0:T(8,128)(2,1)} copy(bf16[1,64,2048]{2,1,0:T(8,128)(2,1)S(1)} %shard_map.37) | data formatting | bytes 524288
Async XLA Ops:
  0.0 0.9 %copy-start = (bf16[1,64,2048]{2,1,0:T(8,128)(2,1)S(1)}, bf16[1,64,2048]{2,1,0:T(8,128)(2,1)}, u32[]{:S(2)}) copy-start(bf16[1,64,2048]{2,1,0:T(8,128)(2,1)} %q_in.1) | copy-start | bytes 786436
  1.0 0.9 %copy-start.1 = (bf16[1,64,1024]{2,1,0:T(8,128)(2,1)S(1)}, bf16[1,64,1024]{2,1,0:T(8,128)(2,1)}, u32[]{:S(2)}) copy-start(bf16[1,64,1024]{2,1,0:T(8,128)(2,1)} %kv_in.1) | copy-start | bytes 393220
  1.9 0.7 %copy-start.2 = (s32[1,64]{1,0:T(1,128)S(1)}, s32[1,64]{1,0:T(1,128)}, u32[]{:S(2)}) copy-start(s32[1,64]{1,0:T(1,128)} %seg_in.1) | copy-start | bytes 772

commit v3 on v2

--- a/solution.py
+++ b/solution.py
@@ -11,7 +11,7 @@
 HEAD_SIZE = 128
 MASKED = -1e30
 MESH = pl.DeviceIdType.MESH
-RIGHT, DOWN, LEFT, OWN = range(4)
+OWN, RIGHT, RIGHT2, DOWN, LEFT, LEFT2 = range(6)
 PIECES = 2
 
 
@@ -24,36 +24,25 @@
     rows = q.shape[0]
     me = x * columns + z
     count = blocks * columns
-    has_right, has_left = z < columns - 1, z > 0
     has_down, has_up = x < blocks - 1, x > 0
-    below = x > 0
+    both = jnp.logical_and
+    near = lambda step: both(z + step >= 0, z + step < columns)
 
     barrier = pltpu.get_barrier_semaphore()
 
-    def greet(section, blk, head):
-        pl.semaphore_signal(barrier, inc=1, device_id=(section, blk, head), device_id_type=MESH)
-
-    greet(before, x, z)
-
-    @pl.when(has_left)
-    def _():
-        greet(before, x, z - 1)
-        greet(s, x, z - 1)
-
-    @pl.when(has_up)
-    def _():
-        greet(before, x - 1, z)
-        greet(s, x - 1, z)
-
-    @pl.when(jnp.logical_and(below, has_right))
-    def _():
-        greet(s, x, z + 1)
-
-    one = lambda c: jnp.where(c, 1, 0)
-    pl.semaphore_wait(
-        barrier,
-        1 + 2 * one(has_right) + 2 * one(has_down) + one(jnp.logical_and(below, has_left)),
-    )
+    def greet(condition, section, blk, head):
+        @pl.when(condition)
+        def _():
+            pl.semaphore_signal(barrier, inc=1, device_id=(section, blk, head), device_id_type=MESH)
+
+    greet(s >= 0, before, x, z)
+    greet(has_up, s, x - 1, z)
+    targets = 1 + jnp.where(has_down, 1, 0)
+    for step in (1, 2):
+        greet(near(-step), s, x, z - step)
+        greet(both(has_up, near(step)), s, x, z + step)
+        targets += jnp.where(near(step), 1, 0) + jnp.where(both(has_up, near(-step)), 1, 0)
+    pl.semaphore_wait(barrier, targets)
 
     width = kv.shape[2] // PIECES
 
@@ -74,17 +63,6 @@
         for copy in copies(OWN, slot, piece, (after, x, z)):
             copy.wait_recv()
 
-    def passing(condition, act, way, slot, piece, device, first=False):
-        @pl.when(condition)
-        def _():
-            for copy in copies(way, slot, piece, device, first):
-                act(copy)
-
-    def first_hops(act):
-        for piece in range(PIECES):
-            passing(has_right, act, RIGHT, me, piece, (after, x, z + 1), True)
-            passing(has_down, act, DOWN, me, piece, (after, x + 1, z), True)
-
     query_copy = pltpu.make_async_remote_copy(
         src_ref=q_in.at[0], dst_ref=q, send_sem=q_send, recv_sem=q_recv,
         device_id=(after, x, z), device_id_type=MESH,
@@ -94,45 +72,41 @@
         for piece in range(PIECES):
             for copy in copies(OWN, me, piece, (after, x, z), True):
                 act(copy)
-        act(query_copy)
-
-    def rounds(act, wait):
-        right, down, left = (s, x, z + 1), (s, x + 1, z), (s, x, z - 1)
-        for d in range(columns):
-            for piece in range(PIECES):
-                last = piece == PIECES - 1
+
+    to = {
+        RIGHT: (s, x, z + 1), RIGHT2: (s, x, z + 2), DOWN: (s, x + 1, z), LEFT: (s, x, z - 1), LEFT2: (s, x, z - 2),
+    }
+    arrivals = []
+    for d in range(columns):
+        for piece in range(PIECES):
+            last = piece == PIECES - 1
+            inner = both(has_down, z > d) if last and d > 0 else has_down
+            sends = [(inner, DOWN)]
+            if d != 1:
+                sends.insert(0, (near(1), RIGHT))
+            if d == 0:
+                sends.insert(1, (near(2), RIGHT2))
+            arrivals.append((z >= d, me - d, piece, sends))
+            for e in range(1, blocks):
+                sends = [(inner, DOWN)]
+                if d == 0:
+                    sends += [(near(-1), LEFT), (near(-2), LEFT2)]
+                if last and d != 1:
+                    sends.append((both(near(1), z == d), RIGHT))
+                if last and d == 0:
+                    sends.append((both(near(2), z == 0), RIGHT2))
+                arrivals.append((both(x >= e, z >= d), me - e * columns - d, piece, sends))
                 if d > 0:
-                    @pl.when(z >= d)
-                    def _():
-                        slot = me - d
-                        wait(slot, piece)
-                        passing(has_right, act, RIGHT, slot, piece, right)
-                        passing(jnp.logical_and(has_down, z > d) if last else has_down, act, DOWN, slot, piece, down)
-                for e in range(1, blocks):
-                    @pl.when(jnp.logical_and(x >= e, z >= d))
-                    def _():
-                        slot = me - e * columns - d
-                        wait(slot, piece)
-                        if d == 0:
-                            passing(has_left, act, LEFT, slot, piece, left)
-                            passing(has_down, act, DOWN, slot, piece, down)
-                        else:
-                            passing(
-                                jnp.logical_and(has_down, z > d) if last else has_down,
-                                act, DOWN, slot, piece, down,
-                            )
-                        if last:
-                            passing(jnp.logical_and(has_right, z == d), act, RIGHT, slot, piece, right)
-
-                    if d > 0:
-                        @pl.when(jnp.logical_and(x >= e, z + d < columns))
-                        def _():
-                            slot = me - e * columns + d
-                            wait(slot, piece)
-                            passing(has_left, act, LEFT, slot, piece, left)
-
-    start, sent = (lambda copy: copy.start()), (lambda copy: copy.wait_send())
-    first_hops(start)
+                    sends = [(near(-1), LEFT)] if d > 1 else []
+                    arrivals.append((both(x >= e, z + d < columns), me - e * columns + d, piece, sends))
+
+    def passes(sends):
+        needed = z < 0
+        for condition, _ in sends:
+            needed = jnp.logical_or(needed, condition)
+        return needed
+
+    own_hops(lambda copy: copy.start())
 
     for slot in range(1, count):
         @pl.when(slot > me)
@@ -140,11 +114,22 @@
             kv[slot] = jnp.zeros(kv.shape[1:], kv.dtype)
             seg[slot] = jnp.zeros(seg.shape[1:], seg.dtype)
 
-    first_hops(sent)
-    own_hops(start)
-    rounds(start, wait_piece)
-    for piece in range(PIECES):
-        wait_piece(me, piece)
+    for n, (valid, slot, piece, sends) in enumerate(arrivals):
+        if sends:
+            @pl.when(both(valid, passes(sends)))
+            def _():
+                wait_piece(slot, piece)
+                for condition, way in sends:
+                    @pl.when(condition)
+                    def _():
+                        for copy in copies(way, slot, piece, to[way]):
+                            copy.start()
+        if n == 0:
+            query_copy.start()
+    for valid, slot, piece, sends in arrivals:
+        @pl.when(both(valid, jnp.logical_not(passes(sends))))
+        def _():
+            wait_piece(slot, piece)
     query_copy.wait_recv()
 
     span = count * rows
@@ -183,14 +168,23 @@
             h = group * k + g
             out_ref[0, :, h * HEAD_SIZE : (h + 1) * HEAD_SIZE] = mixed[g * rows : (g + 1) * rows]
 
-    own_hops(sent)
-    rounds(sent, lambda slot, piece: None)
+    own_hops(lambda copy: copy.wait_send())
+    query_copy.wait_send()
+    for valid, slot, piece, sends in arrivals:
+        for condition, way in sends:
+            @pl.when(both(valid, condition))
+            def _():
+                for copy in copies(way, slot, piece, to[way]):
+                    copy.wait_send()
 
 
 def per_device(queries, keys_values, segment_ids):
     sections, blocks, columns = (lax.axis_size(a) for a in ("section", "blk", "head"))
     rows = queries.shape[1]
     count = blocks * columns
+    queries, keys_values, segment_ids = (
+        pltpu.with_memory_space_constraint(a, pltpu.HBM) for a in (queries, keys_values, segment_ids)
+    )
     return pl.pallas_call(
         functools.partial(kernel, sections, blocks, columns),
         out_shape=jax.ShapeDtypeStruct(queries.shape, jnp.bfloat16),
@@ -202,9 +196,9 @@
             pltpu.VMEM((count, 1, rows), jnp.int32),
             pltpu.SemaphoreType.DMA,
             pltpu.SemaphoreType.DMA,
-            pltpu.SemaphoreType.DMA((4, count, PIECES)),
+            pltpu.SemaphoreType.DMA((6, count, PIECES)),
             pltpu.SemaphoreType.DMA((count, PIECES)),
-            pltpu.SemaphoreType.DMA((4, count)),
+            pltpu.SemaphoreType.DMA((6, count)),
             pltpu.SemaphoreType.DMA((count,)),
         ],
         compiler_params=pltpu.CompilerParams(

time: 24.5 us -> 22.6 us (0.922)
  local copies, waits for them, and re-layouts: 3.21 us -> 0.71 us
  Pallas kernels: 21.1 us -> 21.7 us
    unnamed x7 -> x1, local copies, waits for them, and re-layouts: 3.21 us -> 0.71 us
    pallas_call x1, Pallas kernels: 21.1 us -> 21.7 us  [per_device(): pl.pallas_call(functools.partial(kernel, sections, blocks, columns), out_...]
where the time goes in v3:
time: 22.6 us; the launch traced here: 22.4 us
  Pallas kernels  21.7 us (96%)
  local copies, waits for them, and re-layouts  0.71 us (3%)
    pallas_call x1, Pallas kernels, per_device(): pl.pallas_call(functools.partial(kernel, sections, blocks, columns), out_...  21.7 us
    unnamed x1, local copies, waits for them, and re-layouts  0.71 us

profile of v3, /device:TPU:2, one launch (start us, length us, event | category | flops | bytes accessed | tf_op | source)
XLA Modules:
  0.0 22.4 jit_solution(9860079816605941266)
XLA Ops:
  0.0 21.7 %shard_map.37 = bf16[1,64,2048]{2,1,0:T(8,128)(2,1)S(1)} custom-call(bf16[1,64,2048]{2,1,0:T(8,128)(2,1)} %q_in.1, bf16[1,64,1024]{2,1,0:T(8,128)(2,1)} %kv_in.1, s32[1,64]{1,0:T(1,128)} %seg_in.1), custom_call_target="tpu_custom_call" | custom-call | tf_op jit(solution)/shard_map/pallas_call | solution.py:188
  21.7 0.7 %copy.5 = bf16[1,64,2048]{2,1,0:T(8,128)(2,1)} copy(bf16[1,64,2048]{2,1,0:T(8,128)(2,1)S(1)} %shard_map.37) | data formatting | bytes 524288

commit v4 on v3

--- a/solution.py
+++ b/solution.py
@@ -11,7 +11,7 @@
 HEAD_SIZE = 128
 MASKED = -1e30
 MESH = pl.DeviceIdType.MESH
-OWN, RIGHT, RIGHT2, DOWN, LEFT, LEFT2 = range(6)
+OWN, RIGHT, DOWN, LEFT = range(4)
 PIECES = 2
 
 
@@ -36,12 +36,12 @@
             pl.semaphore_signal(barrier, inc=1, device_id=(section, blk, head), device_id_type=MESH)
 
     greet(s >= 0, before, x, z)
-    greet(has_up, s, x - 1, z)
-    targets = 1 + jnp.where(has_down, 1, 0)
-    for step in (1, 2):
-        greet(near(-step), s, x, z - step)
-        greet(both(has_up, near(step)), s, x, z + step)
-        targets += jnp.where(near(step), 1, 0) + jnp.where(both(has_up, near(-step)), 1, 0)
+    for section in (before, s):
+        greet(has_up, section, x - 1, z)
+        greet(near(-1), section, x, z - 1)
+    greet(both(has_up, near(1)), s, x, z + 1)
+    one = lambda condition: jnp.where(condition, 1, 0)
+    targets = 1 + 2 * one(has_down) + 2 * one(near(1)) + one(both(has_up, near(-1)))
     pl.semaphore_wait(barrier, targets)
 
     width = kv.shape[2] // PIECES
@@ -73,32 +73,33 @@
             for copy in copies(OWN, me, piece, (after, x, z), True):
                 act(copy)
 
-    to = {
-        RIGHT: (s, x, z + 1), RIGHT2: (s, x, z + 2), DOWN: (s, x + 1, z), LEFT: (s, x, z - 1), LEFT2: (s, x, z - 2),
-    }
+    def first_hops(act):
+        for piece in range(PIECES):
+            for condition, way, device in ((near(1), RIGHT, (after, x, z + 1)), (has_down, DOWN, (after, x + 1, z))):
+                @pl.when(condition)
+                def _():
+                    for copy in copies(way, me, piece, device, True):
+                        act(copy)
+
+    to = {RIGHT: (s, x, z + 1), DOWN: (s, x + 1, z), LEFT: (s, x, z - 1)}
     arrivals = []
     for d in range(columns):
         for piece in range(PIECES):
             last = piece == PIECES - 1
             inner = both(has_down, z > d) if last and d > 0 else has_down
-            sends = [(inner, DOWN)]
-            if d != 1:
-                sends.insert(0, (near(1), RIGHT))
-            if d == 0:
-                sends.insert(1, (near(2), RIGHT2))
+            sends = [(near(1), RIGHT), (inner, DOWN)] if d > 0 else []
             arrivals.append((z >= d, me - d, piece, sends))
             for e in range(1, blocks):
                 sends = [(inner, DOWN)]
                 if d == 0:
-                    sends += [(near(-1), LEFT), (near(-2), LEFT2)]
-                if last and d != 1:
+                    sends.append((near(-1), LEFT))
+                if last:
                     sends.append((both(near(1), z == d), RIGHT))
-                if last and d == 0:
-                    sends.append((both(near(2), z == 0), RIGHT2))
                 arrivals.append((both(x >= e, z >= d), me - e * columns - d, piece, sends))
                 if d > 0:
-                    sends = [(near(-1), LEFT)] if d > 1 else []
-                    arrivals.append((both(x >= e, z + d < columns), me - e * columns + d, piece, sends))
+                    arrivals.append(
+                        (both(x >= e, z + d < columns), me - e * columns + d, piece, [(near(-1), LEFT)])
+                    )
 
     def passes(sends):
         needed = z < 0
@@ -106,7 +107,7 @@
             needed = jnp.logical_or(needed, condition)
         return needed
 
-    own_hops(lambda copy: copy.start())
+    first_hops(lambda copy: copy.start())
 
     for slot in range(1, count):
         @pl.when(slot > me)
@@ -114,7 +115,10 @@
             kv[slot] = jnp.zeros(kv.shape[1:], kv.dtype)
             seg[slot] = jnp.zeros(seg.shape[1:], seg.dtype)
 
-    for n, (valid, slot, piece, sends) in enumerate(arrivals):
+    first_hops(lambda copy: copy.wait_send())
+    own_hops(lambda copy: copy.start())
+    query_copy.start()
+    for valid, slot, piece, sends in arrivals:
         if sends:
             @pl.when(both(valid, passes(sends)))
             def _():
@@ -124,13 +128,16 @@
                     def _():
                         for copy in copies(way, slot, piece, to[way]):
                             copy.start()
-        if n == 0:
-            query_copy.start()
-    for valid, slot, piece, sends in arrivals:
-        @pl.when(both(valid, jnp.logical_not(passes(sends))))
-        def _():
-            wait_piece(slot, piece)
+
+    def wait_rest(which):
+        for valid, slot, piece, sends in arrivals:
+            if piece == which:
+                @pl.when(both(valid, jnp.logical_not(passes(sends))))
+                def _():
+                    wait_piece(slot, piece)
+
     query_copy.wait_recv()
+    wait_rest(0)
 
     span = count * rows
     key_labels = jnp.concatenate([seg[slot] for slot in range(count)], axis=1)
@@ -150,6 +157,8 @@
     bias = jnp.where(allowed, 0.0, MASKED)
     bias = jnp.concatenate([bias] * group, axis=0)
     for k in range(key_heads):
+        if k > 0 and k % (key_heads // PIECES) == 0:
+            wait_rest(k // (key_heads // PIECES))
         at = 2 * k * HEAD_SIZE
         keys = kv[:, :, at : at + HEAD_SIZE].reshape(span, HEAD_SIZE)
         values = kv[:, :, at + HEAD_SIZE : at + 2 * HEAD_SIZE].reshape(span, HEAD_SIZE)
@@ -196,9 +205,9 @@
             pltpu.VMEM((count, 1, rows), jnp.int32),
             pltpu.SemaphoreType.DMA,
             pltpu.SemaphoreType.DMA,
-            pltpu.SemaphoreType.DMA((6, count, PIECES)),
+            pltpu.SemaphoreType.DMA((4, count, PIECES)),
             pltpu.SemaphoreType.DMA((count, PIECES)),
-            pltpu.SemaphoreType.DMA((6, count)),
+            pltpu.SemaphoreType.DMA((4, count)),
             pltpu.SemaphoreType.DMA((count,)),
         ],
         compiler_params=pltpu.CompilerParams(

time: 22.6 us -> 21.7 us (0.960)
  Pallas kernels: 21.7 us -> 20.9 us
    pallas_call x1, Pallas kernels: 21.7 us -> 20.9 us  [per_device(): pl.pallas_call(functools.partial(kernel, sections, blocks, columns), out_...]
where the time goes in v4:
time: 21.7 us; the launch traced here: 21.6 us
  Pallas kernels  20.9 us (96%)
  local copies, waits for them, and re-layouts  0.71 us (3%)
    pallas_call x1, Pallas kernels, per_device(): pl.pallas_call(functools.partial(kernel, sections, blocks, columns), out_...  20.9 us
    unnamed x1, local copies, waits for them, and re-layouts  0.71 us

profile of v4, /device:TPU:2, one launch (start us, length us, event | category | flops | bytes accessed | tf_op | source)
XLA Modules:
  0.0 21.6 jit_solution(11872970225818955524)
XLA Ops:
  0.0 20.9 %shard_map.37 = bf16[1,64,2048]{2,1,0:T(8,128)(2,1)S(1)} custom-call(bf16[1,64,2048]{2,1,0:T(8,128)(2,1)} %q_in.1, bf16[1,64,1024]{2,1,0:T(8,128)(2,1)} %kv_in.1, s32[1,64]{1,0:T(1,128)} %seg_in.1), custom_call_target="tpu_custom_call" | custom-call | tf_op jit(solution)/shard_map/pallas_call | solution.py:197
  20.9 0.7 %copy.5 = bf16[1,64,2048]{2,1,0:T(8,128)(2,1)} copy(bf16[1,64,2048]{2,1,0:T(8,128)(2,1)S(1)} %shard_map.37) | data formatting | bytes 524288

commit v5 on v4

v5 whole, which is shorter than its diff:
```python
import functools
import math

import jax
import jax.numpy as jnp
from jax import lax
from jax.experimental import pallas as pl
from jax.experimental.pallas import tpu as pltpu
from jax.sharding import PartitionSpec as P

HEAD_SIZE = 128
MASKED = -1e30
MESH = pl.DeviceIdType.MESH
OWN, RIGHT, DOWN, LEFT = range(4)
PIECES = 2
LAST = PIECES - 1


def kernel(
    sections, blocks, columns, q_in, kv_in, seg_in, out_ref,
    q, kv, seg, tops, totals, mixes, q_send, q_recv, kv_send, kv_recv, seg_send, seg_recv,
):
    s, x, z = lax.axis_index("section"), lax.axis_index("blk"), lax.axis_index("head")
    after, before = lax.rem(s + 1, sections), lax.rem(s + sections - 1, sections)
    rows = q.shape[0]
    me = x * columns + z
    count = blocks * columns
    has_down, has_up = x < blocks - 1, x > 0
    both, either = jnp.logical_and, jnp.logical_or
    near = lambda step: both(z + step >= 0, z + step < columns)

    barrier = pltpu.get_barrier_semaphore()

    def greet(condition, section, blk, head):
        @pl.when(condition)
        def _():
            pl.semaphore_signal(barrier, inc=1, device_id=(section, blk, head), device_id_type=MESH)

    greet(s >= 0, before, x, z)
    for section in (before, s):
        greet(has_up, section, x - 1, z)
        greet(near(-1), section, x, z - 1)
    greet(near(1), s, x, z + 1)
    greet(both(has_down, near(1)), before, x, z + 1)
    one = lambda condition: jnp.where(condition, 1, 0)
    targets = 1 + 2 * one(has_down) + 2 * one(near(1)) + one(near(-1)) + one(both(has_down, near(-1)))
    pl.semaphore_wait(barrier, targets)

    width = kv.shape[2] // PIECES

    def copies(way, slot, piece, device, first=False):
        part = pl.ds(piece * width, width)
        src = kv_in.at[0, :, part] if first else kv.at[slot, :, part]
        yield pltpu.make_async_remote_copy(
            src_ref=src, dst_ref=kv.at[slot, :, part], send_sem=kv_send.at[way, slot, piece],
            recv_sem=kv_recv.at[slot, piece], device_id=device, device_id_type=MESH,
        )
        if piece == 0:
            yield pltpu.make_async_remote_copy(
                src_ref=seg_in if first else seg.at[slot], dst_ref=seg.at[slot], send_sem=seg_send.at[way, slot],
                recv_sem=seg_recv.at[slot], device_id=device, device_id_type=MESH,
            )

    def wait_piece(slot, piece):
        for copy in copies(OWN, slot, piece, (after, x, z)):
            copy.wait_recv()

    query_copy = pltpu.make_async_remote_copy(
        src_ref=q_in.at[0], dst_ref=q, send_sem=q_send, recv_sem=q_recv,
        device_id=(after, x, z), device_id_type=MESH,
    )

    def own_hops(act):
        for piece in range(PIECES):
            for copy in copies(OWN, me, piece, (after, x, z), True):
                act(copy)

    def first_hops(act):
        for piece in range(PIECES):
            hops = [(near(1), RIGHT, (after, x, z + 1)), (has_down, DOWN, (after, x + 1, z))]
            if piece == LAST:
                hops.append((both(has_down, near(-1)), LEFT, (after, x, z - 1)))
            for condition, way, device in hops:
                @pl.when(condition)
                def _():
                    for copy in copies(way, me, piece, device, True):
                        act(copy)

    to = {RIGHT: (s, x, z + 1), DOWN: (s, x + 1, z), LEFT: (s, x, z - 1)}
    arrivals = []
    for d in range(columns):
        for piece in range(PIECES):
            last = piece == LAST
            inner = both(has_down, z > d) if last and d > 0 else has_down
            if d > 0:
                arrivals.append((z >= d, me - d, piece, [(near(1), RIGHT), (inner, DOWN)]))
                if last:
                    arrivals.append((both(has_down, near(d)), me + d, piece, [(near(-1), LEFT), (has_down, DOWN)]))
            for e in range(1, blocks):
                slot = me - e * columns
                sends = [(inner, DOWN)]
                if d == 0 and not last:
                    sends.append((near(-1), LEFT))
                if last:
                    sends.append((both(near(1), z == d), RIGHT))
                arrivals.append((both(x >= e, z >= d), slot - d, piece, sends))
                if d > 0:
                    sends = [(has_down, DOWN)] if last else [(near(-1), LEFT)]
                    arrivals.append((both(x >= e, near(d)), slot + d, piece, sends))

    def pending(e, c, piece):
        if e == 0:
            down = both(has_down, c > 0) if piece == LAST else has_down
            return both(c <= z, jnp.logical_not(both(c < z, either(near(1), down))))
        if piece == LAST:
            level = either(both(has_down, either(c > 0, z == 0)), both(c == 0, near(1)))
            passed = jnp.where(c <= z, one(level), one(has_down))
        else:
            passed = jnp.where(c <= z, one(either(has_down, both(c == z, near(-1)))), one(near(-1)))
        return both(x >= e, passed == 0)

    def passes(sends):
        needed = z < 0
        for condition, _ in sends:
            needed = either(needed, condition)
        return needed

    first_hops(lambda copy: copy.start())

    for slot in range(1, count):
        row, column = slot // columns, slot % columns
        later = both(x == row, z < column)

        @pl.when(either(x < row, later))
        def _():
            kv[slot, :, : LAST * width] = jnp.zeros((rows, LAST * width), kv.dtype)
            seg[slot] = jnp.zeros(seg.shape[1:], seg.dtype)

        @pl.when(either(x < row, both(later, jnp.logical_not(has_down))))
        def _():
            kv[slot, :, LAST * width :] = jnp.zeros((rows, width), kv.dtype)

    first_hops(lambda copy: copy.wait_send())
    own_hops(lambda copy: copy.start())
    query_copy.start()
    for valid, slot, piece, sends in arrivals:
        if sends:
            @pl.when(both(valid, passes(sends)))
            def _():
                wait_piece(slot, piece)
                for condition, way in sends:
                    @pl.when(condition)
                    def _():
                        for copy in copies(way, slot, piece, to[way]):
                            copy.start()

    query_heads = q.shape[1] // HEAD_SIZE
    key_heads = kv.shape[2] // (2 * HEAD_SIZE)
    group = query_heads // key_heads
    factor = math.log2(math.e) / math.sqrt(HEAD_SIZE)
    order = []
    for e in range(0, blocks, 2):
        for d in range(columns):
            pair = []
            for f in range(e, min(e + 2, blocks)):
                back, ahead = lax.rem(z - d + columns, columns), lax.rem(z + d, columns)
                c = back if f == 0 else jnp.where(2 * z < columns, ahead, back)
                pair.append((f, c, lax.rem(x - f + blocks, blocks) * columns + c))
            order.append(pair)

    query_copy.wait_recv()
    for n, pair in enumerate(order):
        for piece in range(PIECES):
            for e, c, slot in pair:
                @pl.when(pending(e, c, piece))
                def _():
                    wait_piece(slot, piece)
            if n == 0 and piece == 0:
                line = lax.broadcasted_iota(jnp.int32, (rows, rows), 0)
                lane = lax.broadcasted_iota(jnp.int32, (rows, rows), 1)
                own = jnp.broadcast_to(seg[me], (rows, rows))
                query_labels = jnp.sum(jnp.where(line == lane, own, 0), axis=1, keepdims=True)
            if piece == 0:
                biases = []
                for _, _, slot in pair:
                    allowed = both(slot * rows + lane <= me * rows + line, seg[slot] == query_labels)
                    biases.append(jnp.where(allowed, 0.0, MASKED))
                bias = jnp.concatenate(biases, axis=1)
                bias = jnp.concatenate([bias] * group, axis=0)
            for k in range(piece * key_heads // PIECES, (piece + 1) * key_heads // PIECES):
                at = 2 * k * HEAD_SIZE
                keys = jnp.concatenate([kv[slot, :, at : at + HEAD_SIZE] for _, _, slot in pair], axis=0)
                values = jnp.concatenate(
                    [kv[slot, :, at + HEAD_SIZE : at + 2 * HEAD_SIZE] for _, _, slot in pair], axis=0
                )
                queries = jnp.concatenate(
                    [q[:, h * HEAD_SIZE : (h + 1) * HEAD_SIZE] for h in range(group * k, group * (k + 1))], axis=0
                )
                scores = lax.dot_general(
                    queries, keys, (((1,), (1,)), ((), ())), preferred_element_type=jnp.float32
                ) + bias
                top = jnp.max(scores, axis=1, keepdims=True)
                if n > 0:
                    before_top = tops[k][:, :1]
                    top = jnp.maximum(before_top, top)
                weights = jnp.exp2((scores - top) * factor)
                mixed = jnp.dot(weights.astype(jnp.bfloat16), values, preferred_element_type=jnp.float32)
                if n > 0:
                    kept = jnp.exp2((before_top - top) * factor)
                    weights += totals[k] * kept
                    mixed += mixes[k] * kept
                if n < len(order) - 1:
                    tops[k] = jnp.broadcast_to(top, tops.shape[1:])
                    totals[k] = weights
                    mixes[k] = mixed
                else:
                    mixed = (mixed / jnp.sum(weights, axis=1, keepdims=True)).astype(jnp.bfloat16)
                    for g in range(group):
                        h = group * k + g
                        out_ref[0, :, h * HEAD_SIZE : (h + 1) * HEAD_SIZE] = mixed[g * rows : (g + 1) * rows]

    own_hops(lambda copy: copy.wait_send())
    query_copy.wait_send()
    for valid, slot, piece, sends in arrivals:
        for condition, way in sends:
            @pl.when(both(valid, condition))
            def _():
                for copy in copies(way, slot, piece, to[way]):
                    copy.wait_send()


def per_device(queries, keys_values, segment_ids):
    sections, blocks, columns = (lax.axis_size(a) for a in ("section", "blk", "head"))
    rows = queries.shape[1]
    count = blocks * columns
    key_heads = keys_values.shape[2] // (2 * HEAD_SIZE)
    stacked = rows * queries.shape[2] // HEAD_SIZE // key_heads
    queries, keys_values, segment_ids = (
        pltpu.with_memory_space_constraint(a, pltpu.HBM) for a in (queries, keys_values, segment_ids)
    )
    return pl.pallas_call(
        functools.partial(kernel, sections, blocks, columns),
        out_shape=jax.ShapeDtypeStruct(queries.shape, jnp.bfloat16),
        in_specs=[pl.BlockSpec(memory_space=pltpu.HBM)] * 3,
        out_specs=pl.BlockSpec(memory_space=pltpu.VMEM),
        scratch_shapes=[
            pltpu.VMEM(queries.shape[1:], jnp.bfloat16),
            pltpu.VMEM((count,) + keys_values.shape[1:], jnp.bfloat16),
            pltpu.VMEM((count, 1, rows), jnp.int32),
            pltpu.VMEM((key_heads, stacked, HEAD_SIZE), jnp.float32),
            pltpu.VMEM((key_heads, stacked, min(blocks, 2) * rows), jnp.float32),
            pltpu.VMEM((key_heads, stacked, HEAD_SIZE), jnp.float32),
            pltpu.SemaphoreType.DMA,
            pltpu.SemaphoreType.DMA,
            pltpu.SemaphoreType.DMA((4, count, PIECES)),
            pltpu.SemaphoreType.DMA((count, PIECES)),
            pltpu.SemaphoreType.DMA((4, count)),
            pltpu.SemaphoreType.DMA((count,)),
        ],
        compiler_params=pltpu.CompilerParams(
            collective_id=0, has_side_effects=True, vmem_limit_bytes=48 * 1024 * 1024
        ),
    )(queries, keys_values, segment_ids)


def solution(mesh):
    return jax.shard_map(
        per_device,
        mesh=mesh,
        in_specs=(
            P("section", ("blk", "head"), None),
            P("section", ("blk", "head"), None),
            P("section", ("blk", "head")),
        ),
        out_specs=P("section", ("blk", "head"), None),
        check_vma=False,
    )
```

time: 21.7 us -> 21.8 us (level)
  the two profiles are of different devices: /device:TPU:2 before, /device:TPU:0 now
where the time goes in v5:
time: 21.8 us; the launch traced here: 21.7 us
  Pallas kernels  21 us (96%)
  local copies, waits for them, and re-layouts  0.71 us (3%)
    pallas_call x1, Pallas kernels, per_device(): pl.pallas_call(functools.partial(kernel, sections, blocks, columns), out_...  21 us
    unnamed x1, local copies, waits for them, and re-layouts  0.71 us

profile of v5, /device:TPU:0, one launch (start us, length us, event | category | flops | bytes accessed | tf_op | source)
XLA Modules:
  0.0 21.7 jit_solution(5609443783407644298)
XLA Ops:
  0.0 21.0 %shard_map.37 = bf16[1,64,2048]{2,1,0:T(8,128)(2,1)S(1)} custom-call(bf16[1,64,2048]{2,1,0:T(8,128)(2,1)} %q_in.1, bf16[1,64,1024]{2,1,0:T(8,128)(2,1)} %kv_in.1, s32[1,64]{1,0:T(1,128)} %seg_in.1), custom_call_target="tpu_custom_call" | custom-call | tf_op jit(solution)/shard_map/pallas_call | solution.py:241
  21.0 0.7 %copy.5 = bf16[1,64,2048]{2,1,0:T(8,128)(2,1)} copy(bf16[1,64,2048]{2,1,0:T(8,128)(2,1)S(1)} %shard_map.37) | data formatting | bytes 524288

commit v6 on v5

--- a/solution.py
+++ b/solution.py
@@ -14,6 +14,7 @@
 OWN, RIGHT, DOWN, LEFT = range(4)
 PIECES = 2
 LAST = PIECES - 1
+BEHIND = 2
 
 
 def kernel(
@@ -87,8 +88,8 @@
                         act(copy)
 
     to = {RIGHT: (s, x, z + 1), DOWN: (s, x + 1, z), LEFT: (s, x, z - 1)}
-    arrivals = []
-    for d in range(columns):
+    rounds = [[] for _ in range(columns)]
+    for d, arrivals in enumerate(rounds):
         for piece in range(PIECES):
             last = piece == LAST
             inner = both(has_down, z > d) if last and d > 0 else has_down
@@ -143,17 +144,6 @@
     first_hops(lambda copy: copy.wait_send())
     own_hops(lambda copy: copy.start())
     query_copy.start()
-    for valid, slot, piece, sends in arrivals:
-        if sends:
-            @pl.when(both(valid, passes(sends)))
-            def _():
-                wait_piece(slot, piece)
-                for condition, way in sends:
-                    @pl.when(condition)
-                    def _():
-                        for copy in copies(way, slot, piece, to[way]):
-                            copy.start()
-
     query_heads = q.shape[1] // HEAD_SIZE
     key_heads = kv.shape[2] // (2 * HEAD_SIZE)
     group = query_heads // key_heads
@@ -166,62 +156,85 @@
                 back, ahead = lax.rem(z - d + columns, columns), lax.rem(z + d, columns)
                 c = back if f == 0 else jnp.where(2 * z < columns, ahead, back)
                 pair.append((f, c, lax.rem(x - f + blocks, blocks) * columns + c))
-            order.append(pair)
-
-    query_copy.wait_recv()
-    for n, pair in enumerate(order):
-        for piece in range(PIECES):
-            for e, c, slot in pair:
-                @pl.when(pending(e, c, piece))
-                def _():
-                    wait_piece(slot, piece)
-            if n == 0 and piece == 0:
-                line = lax.broadcasted_iota(jnp.int32, (rows, rows), 0)
-                lane = lax.broadcasted_iota(jnp.int32, (rows, rows), 1)
-                own = jnp.broadcast_to(seg[me], (rows, rows))
-                query_labels = jnp.sum(jnp.where(line == lane, own, 0), axis=1, keepdims=True)
-            if piece == 0:
-                biases = []
-                for _, _, slot in pair:
-                    allowed = both(slot * rows + lane <= me * rows + line, seg[slot] == query_labels)
-                    biases.append(jnp.where(allowed, 0.0, MASKED))
-                bias = jnp.concatenate(biases, axis=1)
-                bias = jnp.concatenate([bias] * group, axis=0)
-            for k in range(piece * key_heads // PIECES, (piece + 1) * key_heads // PIECES):
-                at = 2 * k * HEAD_SIZE
-                keys = jnp.concatenate([kv[slot, :, at : at + HEAD_SIZE] for _, _, slot in pair], axis=0)
-                values = jnp.concatenate(
-                    [kv[slot, :, at + HEAD_SIZE : at + 2 * HEAD_SIZE] for _, _, slot in pair], axis=0
-                )
-                queries = jnp.concatenate(
-                    [q[:, h * HEAD_SIZE : (h + 1) * HEAD_SIZE] for h in range(group * k, group * (k + 1))], axis=0
-                )
-                scores = lax.dot_general(
-                    queries, keys, (((1,), (1,)), ((), ())), preferred_element_type=jnp.float32
-                ) + bias
-                top = jnp.max(scores, axis=1, keepdims=True)
-                if n > 0:
-                    before_top = tops[k][:, :1]
-                    top = jnp.maximum(before_top, top)
-                weights = jnp.exp2((scores - top) * factor)
-                mixed = jnp.dot(weights.astype(jnp.bfloat16), values, preferred_element_type=jnp.float32)
-                if n > 0:
-                    kept = jnp.exp2((before_top - top) * factor)
-                    weights += totals[k] * kept
-                    mixed += mixes[k] * kept
-                if n < len(order) - 1:
-                    tops[k] = jnp.broadcast_to(top, tops.shape[1:])
+            needed = either(x >= e + 1, both(x >= e, z >= d if e == 0 else x >= e))
+            order.append((needed, pair))
+
+    line = lax.broadcasted_iota(jnp.int32, (rows, rows), 0)
+    lane = lax.broadcasted_iota(jnp.int32, (rows, rows), 1)
+
+    def attend(n):
+        needed, pair = order[n]
+
+        @pl.when(needed)
+        def _():
+            for piece in range(PIECES):
+                for e, c, slot in pair:
+                    @pl.when(pending(e, c, piece))
+                    def _():
+                        wait_piece(slot, piece)
+                if piece == 0:
+                    own = jnp.broadcast_to(seg[me], (rows, rows))
+                    labels = jnp.sum(jnp.where(line == lane, own, 0), axis=1, keepdims=True)
+                    biases = []
+                    for _, _, slot in pair:
+                        allowed = both(slot * rows + lane <= me * rows + line, seg[slot] == labels)
+                        biases.append(jnp.where(allowed, 0.0, MASKED))
+                    bias = jnp.concatenate(biases, axis=1)
+                    bias = jnp.concatenate([bias] * group, axis=0)
+                for k in range(piece * key_heads // PIECES, (piece + 1) * key_heads // PIECES):
+                    at = 2 * k * HEAD_SIZE
+                    keys = jnp.concatenate([kv[slot, :, at : at + HEAD_SIZE] for _, _, slot in pair], axis=0)
+                    values = jnp.concatenate(
+                        [kv[slot, :, at + HEAD_SIZE : at + 2 * HEAD_SIZE] for _, _, slot in pair], axis=0
+                    )
+                    heads = range(group * k, group * (k + 1))
+                    queries = jnp.concatenate([q[:, h * HEAD_SIZE : (h + 1) * HEAD_SIZE] for h in heads], axis=0)
+                    scores = lax.dot_general(
+                        queries, keys, (((1,), (1,)), ((), ())), preferred_element_type=jnp.float32
+                    ) + bias
+                    top = jnp.broadcast_to(jnp.max(scores, axis=1, keepdims=True), scores.shape)
+                    if n > 0:
+                        before_top = tops[k]
+                        top = jnp.maximum(before_top, top)
+                    weights = jnp.exp2((scores - top) * factor)
+                    mixed = jnp.dot(weights.astype(jnp.bfloat16), values, preferred_element_type=jnp.float32)
+                    if n > 0:
+                        kept = jnp.exp2((before_top - top) * factor)
+                        weights += totals[k] * kept
+                        mixed += mixes[k] * kept
+                    tops[k] = top
                     totals[k] = weights
                     mixes[k] = mixed
-                else:
-                    mixed = (mixed / jnp.sum(weights, axis=1, keepdims=True)).astype(jnp.bfloat16)
-                    for g in range(group):
-                        h = group * k + g
-                        out_ref[0, :, h * HEAD_SIZE : (h + 1) * HEAD_SIZE] = mixed[g * rows : (g + 1) * rows]
+
+    done = 0
+    for d, arrivals in enumerate(rounds):
+        for valid, slot, piece, sends in arrivals:
+            @pl.when(both(valid, passes(sends)))
+            def _():
+                wait_piece(slot, piece)
+                for condition, way in sends:
+                    @pl.when(condition)
+                    def _():
+                        for copy in copies(way, slot, piece, to[way]):
+                            copy.start()
+        if blocks <= 2 and d >= BEHIND:
+            if done == 0:
+                query_copy.wait_recv()
+            attend(done)
+            done += 1
+    if done == 0:
+        query_copy.wait_recv()
+    for n in range(done, len(order)):
+        attend(n)
+    for k in range(key_heads):
+        mixed = (mixes[k] / jnp.sum(totals[k], axis=1, keepdims=True)).astype(jnp.bfloat16)
+        for g in range(group):
+            h = group * k + g
+            out_ref[0, :, h * HEAD_SIZE : (h + 1) * HEAD_SIZE] = mixed[g * rows : (g + 1) * rows]
 
     own_hops(lambda copy: copy.wait_send())
     query_copy.wait_send()
-    for valid, slot, piece, sends in arrivals:
+    for valid, slot, piece, sends in sum(rounds, []):
         for condition, way in sends:
             @pl.when(both(valid, condition))
             def _():
@@ -247,7 +260,7 @@
             pltpu.VMEM(queries.shape[1:], jnp.bfloat16),
             pltpu.VMEM((count,) + keys_values.shape[1:], jnp.bfloat16),
             pltpu.VMEM((count, 1, rows), jnp.int32),
-            pltpu.VMEM((key_heads, stacked, HEAD_SIZE), jnp.float32),
+            pltpu.VMEM((key_heads, stacked, min(blocks, 2) * rows), jnp.float32),
             pltpu.VMEM((key_heads, stacked, min(blocks, 2) * rows), jnp.float32),
             pltpu.VMEM((key_heads, stacked, HEAD_SIZE), jnp.float32),
             pltpu.SemaphoreType.DMA,

time: 21.8 us -> 20.7 us (0.950)
  the two profiles are of different devices: /device:TPU:0 before, /device:TPU:2 now
where the time goes in v6:
time: 20.7 us; the launch traced here: 20.6 us
  Pallas kernels  19.8 us (96%)
  local copies, waits for them, and re-layouts  0.71 us (3%)
    pallas_call x1, Pallas kernels, per_device(): pl.pallas_call(functools.partial(kernel, sections, blocks, columns), out_...  19.8 us
    unnamed x1, local copies, waits for them, and re-layouts  0.71 us

profile of v6, /device:TPU:2, one launch (start us, length us, event | category | flops | bytes accessed | tf_op | source)
XLA Modules:
  0.0 20.6 jit_solution(10866463655170143014)
XLA Ops:
  0.0 19.8 %shard_map.37 = bf16[1,64,2048]{2,1,0:T(8,128)(2,1)S(1)} custom-call(bf16[1,64,2048]{2,1,0:T(8,128)(2,1)} %q_in.1, bf16[1,64,1024]{2,1,0:T(8,128)(2,1)} %kv_in.1, s32[1,64]{1,0:T(1,128)} %seg_in.1), custom_call_target="tpu_custom_call" | custom-call | tf_op jit(solution)/shard_map/pallas_call | solution.py:254
  19.9 0.7 %copy.5 = bf16[1,64,2048]{2,1,0:T(8,128)(2,1)} copy(bf16[1,64,2048]{2,1,0:T(8,128)(2,1)S(1)} %shard_map.37) | data formatting | bytes 524288

commit v7 on v6

--- a/solution.py
+++ b/solution.py
@@ -43,6 +43,7 @@
         greet(near(-1), section, x, z - 1)
     greet(near(1), s, x, z + 1)
     greet(both(has_down, near(1)), before, x, z + 1)
+    direct, relayed = lax.rem(s, 2) == 0, lax.rem(before, 2) == 1
     one = lambda condition: jnp.where(condition, 1, 0)
     targets = 1 + 2 * one(has_down) + 2 * one(near(1)) + one(near(-1)) + one(both(has_down, near(-1)))
     pl.semaphore_wait(barrier, targets)
@@ -82,7 +83,7 @@
             if piece == LAST:
                 hops.append((both(has_down, near(-1)), LEFT, (after, x, z - 1)))
             for condition, way, device in hops:
-                @pl.when(condition)
+                @pl.when(both(direct, condition))
                 def _():
                     for copy in copies(way, me, piece, device, True):
                         act(copy)
@@ -93,7 +94,12 @@
         for piece in range(PIECES):
             last = piece == LAST
             inner = both(has_down, z > d) if last and d > 0 else has_down
-            if d > 0:
+            if d == 0:
+                sends = [(both(relayed, near(1)), RIGHT), (both(relayed, has_down), DOWN)]
+                if last:
+                    sends.append((both(relayed, both(has_down, near(-1))), LEFT))
+                arrivals.append((z >= 0, me, piece, sends))
+            else:
                 arrivals.append((z >= d, me - d, piece, [(near(1), RIGHT), (inner, DOWN)]))
                 if last:
                     arrivals.append((both(has_down, near(d)), me + d, piece, [(near(-1), LEFT), (has_down, DOWN)]))
@@ -112,7 +118,8 @@
     def pending(e, c, piece):
         if e == 0:
             down = both(has_down, c > 0) if piece == LAST else has_down
-            return both(c <= z, jnp.logical_not(both(c < z, either(near(1), down))))
+            passed = jnp.where(c < z, one(either(near(1), down)), one(both(relayed, either(near(1), has_down))))
+            return both(c <= z, passed == 0)
         if piece == LAST:
             level = either(both(has_down, either(c > 0, z == 0)), both(c == 0, near(1)))
             passed = jnp.where(c <= z, one(level), one(has_down))
@@ -127,6 +134,7 @@
         return needed
 
     first_hops(lambda copy: copy.start())
+    own_hops(lambda copy: copy.start())
 
     for slot in range(1, count):
         row, column = slot // columns, slot % columns
@@ -141,8 +149,7 @@
         def _():
             kv[slot, :, LAST * width :] = jnp.zeros((rows, width), kv.dtype)
 
-    first_hops(lambda copy: copy.wait_send())
-    own_hops(lambda copy: copy.start())
+    own_hops(lambda copy: copy.wait_send())
     query_copy.start()
     query_heads = q.shape[1] // HEAD_SIZE
     key_heads = kv.shape[2] // (2 * HEAD_SIZE)
@@ -232,7 +239,7 @@
             h = group * k + g
             out_ref[0, :, h * HEAD_SIZE : (h + 1) * HEAD_SIZE] = mixed[g * rows : (g + 1) * rows]
 
-    own_hops(lambda copy: copy.wait_send())
+    first_hops(lambda copy: copy.wait_send())
     query_copy.wait_send()
     for valid, slot, piece, sends in sum(rounds, []):
         for condition, way in sends:

time: 20.7 us -> 23.4 us (1.13)
  Pallas kernels: 19.8 us -> 22.6 us
    pallas_call x1, Pallas kernels: 19.8 us -> 22.6 us  [per_device(): pl.pallas_call(functools.partial(kernel, sections, blocks, columns), out_...]
where the time goes in v7:
time: 23.4 us; the launch traced here: 23.3 us
  Pallas kernels  22.6 us (97%)
  local copies, waits for them, and re-layouts  0.71 us (3%)
    pallas_call x1, Pallas kernels, per_device(): pl.pallas_call(functools.partial(kernel, sections, blocks, columns), out_...  22.6 us
    unnamed x1, local copies, waits for them, and re-layouts  0.71 us

profile of v7, /device:TPU:2, one launch (start us, length us, event | category | flops | bytes accessed | tf_op | source)
XLA Modules:
  0.0 23.3 jit_solution(14173526670092670904)
XLA Ops:
  0.0 22.6 %shard_map.37 = bf16[1,64,2048]{2,1,0:T(8,128)(2,1)S(1)} custom-call(bf16[1,64,2048]{2,1,0:T(8,128)(2,1)} %q_in.1, bf16[1,64,1024]{2,1,0:T(8,128)(2,1)} %kv_in.1, s32[1,64]{1,0:T(1,128)} %seg_in.1), custom_call_target="tpu_custom_call" | custom-call | tf_op jit(solution)/shard_map/pallas_call | solution.py:261
  22.6 0.7 %copy.5 = bf16[1,64,2048]{2,1,0:T(8,128)(2,1)} copy(bf16[1,64,2048]{2,1,0:T(8,128)(2,1)S(1)} %shard_map.37) | data formatting | bytes 524288

commit v8 on v6

--- a/solution.py
+++ b/solution.py
@@ -14,7 +14,7 @@
 OWN, RIGHT, DOWN, LEFT = range(4)
 PIECES = 2
 LAST = PIECES - 1
-BEHIND = 2
+BEHIND = 1
 
 
 def kernel(
@@ -127,6 +127,7 @@
         return needed
 
     first_hops(lambda copy: copy.start())
+    own_hops(lambda copy: copy.start())
 
     for slot in range(1, count):
         row, column = slot // columns, slot % columns
@@ -141,8 +142,7 @@
         def _():
             kv[slot, :, LAST * width :] = jnp.zeros((rows, width), kv.dtype)
 
-    first_hops(lambda copy: copy.wait_send())
-    own_hops(lambda copy: copy.start())
+    own_hops(lambda copy: copy.wait_send())
     query_copy.start()
     query_heads = q.shape[1] // HEAD_SIZE
     key_heads = kv.shape[2] // (2 * HEAD_SIZE)
@@ -232,7 +232,7 @@
             h = group * k + g
             out_ref[0, :, h * HEAD_SIZE : (h + 1) * HEAD_SIZE] = mixed[g * rows : (g + 1) * rows]
 
-    own_hops(lambda copy: copy.wait_send())
+    first_hops(lambda copy: copy.wait_send())
     query_copy.wait_send()
     for valid, slot, piece, sends in sum(rounds, []):
         for condition, way in sends:

time: 20.7 us -> 21.7 us (1.048)
  Pallas kernels: 19.8 us -> 20.9 us
    pallas_call x1, Pallas kernels: 19.8 us -> 20.9 us  [per_device(): pl.pallas_call(functools.partial(kernel, sections, blocks, columns), out_...]
where the time goes in v8:
time: 21.7 us; the launch traced here: 21.6 us
  Pallas kernels  20.9 us (96%)
  local copies, waits for them, and re-layouts  0.71 us (3%)
    pallas_call x1, Pallas kernels, per_device(): pl.pallas_call(functools.partial(kernel, sections, blocks, columns), out_...  20.9 us
    unnamed x1, local copies, waits for them, and re-layouts  0.71 us

profile of v8, /device:TPU:2, one launch (start us, length us, event | category | flops | bytes accessed | tf_op | source)
XLA Modules:
  0.0 21.6 jit_solution(10061278669007326408)
XLA Ops:
  0.0 20.9 %shard_map.37 = bf16[1,64,2048]{2,1,0:T(8,128)(2,1)S(1)} custom-call(bf16[1,64,2048]{2,1,0:T(8,128)(2,1)} %q_in.1, bf16[1,64,1024]{2,1,0:T(8,128)(2,1)} %kv_in.1, s32[1,64]{1,0:T(1,128)} %seg_in.1), custom_call_target="tpu_custom_call" | custom-call | tf_op jit(solution)/shard_map/pallas_call | solution.py:254
  20.9 0.7 %copy.5 = bf16[1,64,2048]{2,1,0:T(8,128)(2,1)} copy(bf16[1,64,2048]{2,1,0:T(8,128)(2,1)S(1)} %shard_map.37) | data formatting | bytes 524288

commit v9 on v6

--- a/solution.py
+++ b/solution.py
@@ -14,7 +14,6 @@
 OWN, RIGHT, DOWN, LEFT = range(4)
 PIECES = 2
 LAST = PIECES - 1
-BEHIND = 2
 
 
 def kernel(
@@ -126,7 +125,14 @@
             needed = either(needed, condition)
         return needed
 
+    same_chip = lax.rem(s, 2) == 0
+
+    def last_hops():
+        own_hops(lambda copy: copy.start())
+        query_copy.start()
+
     first_hops(lambda copy: copy.start())
+    pl.when(same_chip)(last_hops)
 
     for slot in range(1, count):
         row, column = slot // columns, slot % columns
@@ -141,9 +147,11 @@
         def _():
             kv[slot, :, LAST * width :] = jnp.zeros((rows, width), kv.dtype)
 
-    first_hops(lambda copy: copy.wait_send())
-    own_hops(lambda copy: copy.start())
-    query_copy.start()
+    @pl.when(jnp.logical_not(same_chip))
+    def _():
+        first_hops(lambda copy: copy.wait_send())
+        last_hops()
+
     query_heads = q.shape[1] // HEAD_SIZE
     key_heads = kv.shape[2] // (2 * HEAD_SIZE)
     group = query_heads // key_heads
@@ -206,8 +214,7 @@
                     totals[k] = weights
                     mixes[k] = mixed
 
-    done = 0
-    for d, arrivals in enumerate(rounds):
+    for arrivals in rounds:
         for valid, slot, piece, sends in arrivals:
             @pl.when(both(valid, passes(sends)))
             def _():
@@ -217,20 +224,18 @@
                     def _():
                         for copy in copies(way, slot, piece, to[way]):
                             copy.start()
-        if blocks <= 2 and d >= BEHIND:
-            if done == 0:
-                query_copy.wait_recv()
-            attend(done)
-            done += 1
-    if done == 0:
-        query_copy.wait_recv()
-    for n in range(done, len(order)):
+    query_copy.wait_recv()
+    for n in range(len(order)):
         attend(n)
     for k in range(key_heads):
         mixed = (mixes[k] / jnp.sum(totals[k], axis=1, keepdims=True)).astype(jnp.bfloat16)
         for g in range(group):
             h = group * k + g
             out_ref[0, :, h * HEAD_SIZE : (h + 1) * HEAD_SIZE] = mixed[g * rows : (g + 1) * rows]
+
+    @pl.when(same_chip)
+    def _():
+        first_hops(lambda copy: copy.wait_send())
 
     own_hops(lambda copy: copy.wait_send())
     query_copy.wait_send()

time: 20.7 us -> 20.7 us (level)
  no operation moved by 1% of the time
where the time goes in v9:
time: 20.7 us; the launch traced here: 20.6 us
  Pallas kernels  19.9 us (96%)
  local copies, waits for them, and re-layouts  0.71 us (3%)
    pallas_call x1, Pallas kernels, per_device(): pl.pallas_call(functools.partial(kernel, sections, blocks, columns), out_...  19.9 us
    unnamed x1, local copies, waits for them, and re-layouts  0.71 us

profile of v9, /device:TPU:2, one launch (start us, length us, event | category | flops | bytes accessed | tf_op | source)
XLA Modules:
  0.0 20.6 jit_solution(1310762547614698652)
XLA Ops:
  0.0 19.9 %shard_map.37 = bf16[1,64,2048]{2,1,0:T(8,128)(2,1)S(1)} custom-call(bf16[1,64,2048]{2,1,0:T(8,128)(2,1)} %q_in.1, bf16[1,64,1024]{2,1,0:T(8,128)(2,1)} %kv_in.1, s32[1,64]{1,0:T(1,128)} %seg_in.1), custom_call_target="tpu_custom_call" | custom-call | tf_op jit(solution)/shard_map/pallas_call | solution.py:259
  19.9 0.7 %copy.5 = bf16[1,64,2048]{2,1,0:T(8,128)(2,1)} copy(bf16[1,64,2048]{2,1,0:T(8,128)(2,1)S(1)} %shard_map.37) | data formatting | bytes 524288

commit v10 on v9

--- a/solution.py
+++ b/solution.py
@@ -11,7 +11,7 @@
 HEAD_SIZE = 128
 MASKED = -1e30
 MESH = pl.DeviceIdType.MESH
-OWN, RIGHT, DOWN, LEFT = range(4)
+OWN, RIGHT, DOWN, LEFT, DIAGONAL = range(5)
 PIECES = 2
 LAST = PIECES - 1
 
@@ -42,8 +42,9 @@
         greet(near(-1), section, x, z - 1)
     greet(near(1), s, x, z + 1)
     greet(both(has_down, near(1)), before, x, z + 1)
+    greet(both(has_up, near(1)), before, x - 1, z + 1)
     one = lambda condition: jnp.where(condition, 1, 0)
-    targets = 1 + 2 * one(has_down) + 2 * one(near(1)) + one(near(-1)) + one(both(has_down, near(-1)))
+    targets = 1 + 2 * one(has_down) + 2 * one(near(1)) + one(near(-1)) + 2 * one(both(has_down, near(-1)))
     pl.semaphore_wait(barrier, targets)
 
     width = kv.shape[2] // PIECES
@@ -80,6 +81,8 @@
             hops = [(near(1), RIGHT, (after, x, z + 1)), (has_down, DOWN, (after, x + 1, z))]
             if piece == LAST:
                 hops.append((both(has_down, near(-1)), LEFT, (after, x, z - 1)))
+            else:
+                hops.append((both(has_down, near(-1)), DIAGONAL, (after, x + 1, z - 1)))
             for condition, way, device in hops:
                 @pl.when(condition)
                 def _():
@@ -99,7 +102,7 @@
             for e in range(1, blocks):
                 slot = me - e * columns
                 sends = [(inner, DOWN)]
-                if d == 0 and not last:
+                if d == 0 and not last and e > 1:
                     sends.append((near(-1), LEFT))
                 if last:
                     sends.append((both(near(1), z == d), RIGHT))
@@ -116,7 +119,8 @@
             level = either(both(has_down, either(c > 0, z == 0)), both(c == 0, near(1)))
             passed = jnp.where(c <= z, one(level), one(has_down))
         else:
-            passed = jnp.where(c <= z, one(either(has_down, both(c == z, near(-1)))), one(near(-1)))
+            level = either(has_down, both(c == z, near(-1))) if e > 1 else has_down
+            passed = jnp.where(c <= z, one(level), one(near(-1)))
         return both(x >= e, passed == 0)
 
     def passes(sends):
@@ -270,9 +274,9 @@
             pltpu.VMEM((key_heads, stacked, HEAD_SIZE), jnp.float32),
             pltpu.SemaphoreType.DMA,
             pltpu.SemaphoreType.DMA,
-            pltpu.SemaphoreType.DMA((4, count, PIECES)),
+            pltpu.SemaphoreType.DMA((5, count, PIECES)),
             pltpu.SemaphoreType.DMA((count, PIECES)),
-            pltpu.SemaphoreType.DMA((4, count)),
+            pltpu.SemaphoreType.DMA((5, count)),
             pltpu.SemaphoreType.DMA((count,)),
         ],
         compiler_params=pltpu.CompilerParams(

time: 20.7 us -> 21.1 us (1.019)
  Pallas kernels: 19.9 us -> 20.3 us
    pallas_call x1, Pallas kernels: 19.9 us -> 20.3 us  [per_device(): pl.pallas_call(functools.partial(kernel, sections, blocks, columns), out_...]
where the time goes in v10:
time: 21.1 us; the launch traced here: 21 us
  Pallas kernels  20.3 us (96%)
  local copies, waits for them, and re-layouts  0.71 us (3%)
    pallas_call x1, Pallas kernels, per_device(): pl.pallas_call(functools.partial(kernel, sections, blocks, columns), out_...  20.3 us
    unnamed x1, local copies, waits for them, and re-layouts  0.71 us

profile of v10, /device:TPU:2, one launch (start us, length us, event | category | flops | bytes accessed | tf_op | source)
XLA Modules:
  0.0 21.0 jit_solution(7570266766642955602)
XLA Ops:
  0.0 20.3 %shard_map.37 = bf16[1,64,2048]{2,1,0:T(8,128)(2,1)S(1)} custom-call(bf16[1,64,2048]{2,1,0:T(8,128)(2,1)} %q_in.1, bf16[1,64,1024]{2,1,0:T(8,128)(2,1)} %kv_in.1, s32[1,64]{1,0:T(1,128)} %seg_in.1), custom_call_target="tpu_custom_call" | custom-call | tf_op jit(solution)/shard_map/pallas_call | solution.py:263
  20.3 0.7 %copy.5 = bf16[1,64,2048]{2,1,0:T(8,128)(2,1)} copy(bf16[1,64,2048]{2,1,0:T(8,128)(2,1)S(1)} %shard_map.37) | data formatting | bytes 524288
